TPU v7x, 32 devices: a whole 2x2x4 slice. The times are simulated.
32 devices in a mesh: band: 16 (over z, y, core), member: 2 (over x).
Axes of the slice: x: 2, y: 2, z: 4, core: 2. Of those that a mesh axis runs over, the one named last changes fastest.
Arguments:
- grid_latent: bfloat16 [2, 16384, 512], P('member', 'band'), may hold values from -6 to 6
- mesh_latent: bfloat16 [2, 16384, 512], P('member', 'band'), may hold values from -6 to 6
- edge_attr: bfloat16 [4, 4, 16384], P(None, None, 'band'), may hold values from -5 to 5
- neighbours: int32 [16384, 4], P('band'), may hold values from 0 to 2047, as said below
- send_rows: int32 [32, 512], P('band'), may hold values from 0 to 1023, as said below
- target: float32 [100, 16384], P(None, 'band'), may hold values from -6 to 6
- field_weight: float32 [100], replicated, may hold values from 1 to 10
- w_src: bfloat16 [512, 512], replicated, may hold values from -0.25 to 0.25
- w_dst: bfloat16 [512, 512], replicated, may hold values from -0.25 to 0.25
- w_edge: bfloat16 [4, 512], replicated, may hold values from -3 to 3
- w_msg: bfloat16 [512, 512], replicated, may hold values from -0.25 to 0.25
- ln_gain: float32 [512], replicated, may hold values from 0.1 to 1.9
- w_out: bfloat16 [512, 100], replicated, may hold values from -0.25 to 0.25
Outputs:
- d_grid: bfloat16 [2, 16384, 512], P('member', 'band')
- d_mesh: bfloat16 [2, 16384, 512], P('member', 'band')
Inputs may be any that keep to these rules, and one draw needn't show every extreme that they name: `neighbours`: grid points of band index 0 never name slots 1024 to 1535, those of the last band index never name slots 1024 + 512 and up. `send_rows`: the two lists of one band index hold 1024 distinct rows together.
All inputs are finite; a program needn't handle non-finite values.
Results may differ from a plain program's by a relative error of at most 0.04.
Values may be sent and summed in bfloat16 or wider, within the bound.
No kernel may reach another device: no remote copies, remote signals or barrier semaphores. Data moves between devices by JAX's collectives and lax.ppermute only.
A program may use at most 128 MiB of HBM per device.

v0:
```python
import functools

import jax
import jax.numpy as jnp
from jax import lax
from jax.experimental import pallas as pl
from jax.experimental.pallas import tpu as pltpu
from jax.sharding import PartitionSpec as P

DELTA_SQ = 0.0625
ALPHA = 0.95
LN_EPS = 1e-05
F32 = jnp.float32
BF16 = jnp.bfloat16
IN_SHADOW = (1, 1)
VMEM_LIMIT = 28 * 1024 * 1024


def slope(diff):
    return diff * lax.rsqrt(diff * diff + DELTA_SQ)


def mm(left, right):
    return jnp.dot(left, right, preferred_element_type=F32)


def mm_t(left, right):
    return lax.dot_general(left, right, (((1,), (1,)), ((), ())), preferred_element_type=F32)


STRIP = 16


def strips(rows, size=STRIP):
    return [slice(first, first + size) for first in range(0, rows, size)]


def column_of(ids):
    lanes = 128
    rows = ids.shape[1]
    column = jnp.broadcast_to(ids.astype(F32), (lanes, rows)).T.astype(jnp.int16)
    return column - lax.broadcasted_iota(jnp.int16, (rows, lanes), 1)


def column_hot(column, base, slots):
    offset = column - jnp.broadcast_to(base, column.shape).astype(jnp.int16)
    parts = [
        jnp.where(offset == jnp.int16(first), BF16(1), BF16(0))
        for first in range(0, slots, column.shape[1])
    ]
    return jnp.concatenate(parts, axis=1)


def fill_rows(hot_ref, ids, base):
    edges, points = ids.shape
    sublane = lax.broadcasted_iota(jnp.int16, (STRIP, points), 0)
    for k in range(edges):
        row = jnp.broadcast_to(ids[k : k + 1, :] - base, (STRIP, points)).astype(jnp.int16)
        offset = row - sublane
        for part in strips(hot_ref.shape[0]):
            hot_ref[part, k * points : (k + 1) * points] = jnp.where(
                offset == jnp.int16(part.start), BF16(1), BF16(0)
            )


def swap(firsts):
    return [pair for i in firsts for pair in ((i, i + 1), (i + 1, i))]


def hbm(array):
    return pltpu.with_memory_space_constraint(array, pltpu.HBM)


def call(body, places, out_places, out_shape, flops, nbytes, scratch=()):
    def specs(memories):
        return [pl.BlockSpec(memory_space=memory) for memory in memories]

    return pl.pallas_call(
        body,
        in_specs=specs(places),
        out_specs=specs(out_places),
        out_shape=out_shape,
        scratch_shapes=scratch,
        compiler_params=pltpu.CompilerParams(vmem_limit_bytes=VMEM_LIMIT),
        cost_estimate=pl.CostEstimate(flops=flops, bytes_accessed=nbytes, transcendentals=0),
    )


def near_far(low, high):
    odd = lax.axis_index("band") % 2 == 1
    return jnp.where(odd, low, high), jnp.where(odd, high, low)


def rim_bases(owned, halo):
    return near_far(owned, owned + halo)


def rows_to(array, rows):
    array = array.astype(F32)
    return jnp.concatenate([array, jnp.zeros((rows - array.shape[0], array.shape[1]), F32)], axis=0)


def pieces(rows, size):
    return [slice(first, first + size) for first in range(0, rows, size)]


def placed_rows(refs):
    first, out = 0, []
    for ref in refs:
        out.append((slice(first, first + ref.shape[0]), ref))
        first += ref.shape[0]
    return out


def join(refs, whole_ref):
    for rows, ref in placed_rows(refs):
        whole_ref[rows, :] = ref[...]


def far_kernel(held, mesh_hbm, w_src_hbm, send_hbm, *refs):
    held_hbm, (far_ref, mesh_ref, w_src_ref, *held_refs) = refs[:held], refs[held:-2]
    send_ref, sems = refs[-2:]
    owned = mesh_ref.shape[0]
    parts = pieces(owned, owned // 2)
    moves = [(send_hbm, send_ref)]
    moves += [(mesh_hbm.at[part], mesh_ref.at[part]) for part in parts]
    moves += [(w_src_hbm, w_src_ref), *zip(held_hbm, held_refs)]
    loads = [pltpu.make_async_copy(*move, sems.at[i]) for i, move in enumerate(moves)]
    for load in loads:
        load.start()
    loads[0].wait()
    far = near_far(send_ref[0:1, :], send_ref[1:2, :])[1]
    column = column_of(far)
    hots = [column_hot(column, part.start, part.stop - part.start) for part in parts]
    rows = None
    for load, part, hot in zip(loads[1:], parts, hots):
        load.wait()
        picked = mm(hot, mesh_ref[part])
        rows = picked if rows is None else rows + picked
    loads[1 + len(parts)].wait()
    far_ref[...] = mm(rows.astype(BF16), w_src_ref[...]).astype(BF16)
    for load in loads[2 + len(parts) :]:
        load.wait()


def near_kernel(mesh_ref, w_src_ref, send_ref, src_ref, *near_refs):
    src = mm(mesh_ref[...], w_src_ref[...]).astype(BF16)
    src_ref[...] = src
    near = near_far(send_ref[0:1, :], send_ref[1:2, :])[0]
    rows = mm(column_hot(column_of(near), 0, src.shape[0]), src_ref[...]).astype(BF16)
    for part, near_ref in placed_rows(near_refs):
        near_ref[...] = rows[part, :]


def own_kernel(
    block,
    slots_ref,
    src_ref,
    grid_ref,
    w_dst_ref,
    attr_ref,
    w_edge_ref,
    *refs,
):
    *near_refs, pre_ref, columns_ref, rows_ref, dst_ref, embed_ref, attr_f32, near_ref = refs
    join(near_refs, near_ref)
    edges, lanes, channels = embed_ref.shape
    feats = w_edge_ref.shape[0]
    row = lax.broadcasted_iota(jnp.int32, (lanes, channels), 0)
    w_edge = w_edge_ref[...].astype(F32)
    for k in range(edges):
        spread = jnp.zeros((lanes, channels), F32)
        for e in range(feats):
            spread = jnp.where(row == e * edges + k, w_edge[e : e + 1, :], spread)
        embed_ref[k] = spread.astype(BF16)
    for e in range(feats):
        attr_f32[e * edges : (e + 1) * edges, :] = attr_ref[e].astype(F32)
    owned = src_ref.shape[0]
    halo = near_ref.shape[0]
    base, far = rim_bases(owned, halo)
    for at, rows in enumerate(pieces(grid_ref.shape[0], block)):
        dst_ref[at] = mm(grid_ref[rows, :], w_dst_ref[...])
        attr = rows_to(attr_f32[:, rows], lanes).T.astype(BF16)
        for k in range(edges):
            column = column_of(slots_ref[k : k + 1, rows])
            picked = mm(column_hot(column, 0, owned), src_ref[...])
            picked = picked + mm(column_hot(column, base, halo), near_ref[...])
            embed = mm(attr, embed_ref[k])
            pre_ref[k, rows, :] = (picked + embed + dst_ref[at]).astype(BF16)
            columns_ref[k, rows, :] = column_hot(column, far, halo)
    chunks, _, width = rows_ref.shape
    part = width // edges
    for c in range(chunks):
        fill_rows(rows_ref.at[c], slots_ref[:, c * part : (c + 1) * part], far)


def forward_kernel(
    first,
    block,
    fields,
    columns_ref,
    pre_ref,
    grid_ref,
    w_msg_ref,
    gain_ref,
    w_out_ref,
    far_ref,
    pred_ref,
    pred_bf_ref,
    sg_ref,
    zhat_ref,
    rstd_ref,
):
    half = BF16(0.5)
    w_out = rows_to(w_out_ref[...], fields).astype(BF16)
    for rows in pieces(zhat_ref.shape[0], block):
        source = slice(first + rows.start, first + rows.stop)
        acts = []
        for k in range(columns_ref.shape[0]):
            picked = mm(columns_ref[k, source, :], far_ref[...])
            pre = pre_ref[k, source, :] + picked.astype(BF16)
            sigma = half + half * jnp.tanh(half * pre)
            act = pre * sigma
            acts.append(act)
            sg_ref[k, rows, :] = sigma + (act - act * sigma)
        while len(acts) > 1:
            acts = [sum(acts[i : i + 2][1:], acts[i]) for i in range(0, len(acts), 2)]
        z = grid_ref[source, :].astype(F32) + mm(acts[0], w_msg_ref[...])
        centre = z - jnp.mean(z, axis=1, keepdims=True)
        rstd = lax.rsqrt(jnp.mean(centre * centre, axis=1, keepdims=True) + LN_EPS)
        zhat = centre * rstd
        pred = mm_t(w_out, (zhat * gain_ref[...]).astype(BF16))
        pred_ref[:, rows] = pred
        pred_bf_ref[:, rows] = pred[: pred_bf_ref.shape[0], :].astype(BF16)
        zhat_ref[rows, :] = zhat.astype(BF16)
        rstd_ref[rows, :] = jnp.broadcast_to(rstd, (block, rstd_ref.shape[1]))


def backward_kernel(
    chunk,
    block,
    coeff,
    given,
    hot_ref,
    pred_ref,
    others_ref,
    target_ref,
    weight_ref,
    w_out_ref,
    gain_ref,
    zhat_ref,
    rstd_ref,
    w_msg_ref,
    sg_ref,
    *refs,
):
    prior, (dz_ref, dpre_ref, far_ref, dpred_ref, wide_ref) = refs[:given], refs[given:]
    fields = pred_ref.shape[0]
    edges, points, channels = dpre_ref.shape
    first = chunk * points
    weight = weight_ref[...]
    weight = jnp.concatenate([weight, jnp.zeros((1, fields - weight.shape[1]), F32)], axis=1)
    w_out = rows_to(w_out_ref[...], fields).astype(BF16)
    gain = gain_ref[...]
    sent = others_ref.shape[1]
    for rows in pieces(points, block):
        for part in strips(block, 128):
            part = slice(rows.start + part.start, rows.start + part.stop)
            pred = pred_ref[:, part]
            spread = jnp.zeros((sent, 128), F32)
            for other in range(others_ref.shape[0]):
                spread = spread + slope(pred[:sent, :] - others_ref[other, :, part].astype(F32))
            target = target_ref[:, first + part.start : first + part.stop]
            d_pred = slope(pred - rows_to(target, fields)) - coeff * rows_to(spread, fields)
            dpred_ref[part, :] = (weight * d_pred.T).astype(BF16)
        wide_ref[rows, :] = mm(dpred_ref[rows, :], w_out)
        for part in strips(block, 32):
            part = slice(rows.start + part.start, rows.start + part.stop)
            scaled = wide_ref[part, :] * gain
            zhat = zhat_ref[part, :].astype(F32)
            d_z = rstd_ref[part, :1] * (
                scaled
                - jnp.mean(scaled, axis=1, keepdims=True)
                - zhat * jnp.mean(scaled * zhat, axis=1, keepdims=True)
            )
            dz_ref[part, :] = d_z.astype(BF16)
        wide_ref[rows, :] = mm_t(dz_ref[rows, :], w_msg_ref[...])
        for part in strips(block):
            part = slice(rows.start + part.start, rows.start + part.stop)
            d_act = wide_ref[part, :].astype(BF16)
            for k in range(edges):
                dpre_ref[k, part, :] = d_act * sg_ref[k, part, :]
    far = mm(hot_ref[chunk], dpre_ref[...].reshape(edges * points, channels))
    if prior:
        far = far + prior[0][...]
    far_ref[...] = far.astype(far_ref.dtype)


def rim_kernel(owned, chunks, slots_ref, *refs):
    dpre_refs = refs[:chunks]
    *near_refs, acc, hot_ref = refs[chunks:]
    base = rim_bases(owned, acc.shape[0])[0]
    first = 0
    for c, dpre_ref in enumerate(dpre_refs):
        edges, points, channels = dpre_ref.shape
        fill_rows(hot_ref.at[c], slots_ref[:, first : first + points], base)
        first += points
        added = mm(hot_ref[c], dpre_ref[...].reshape(edges * points, channels))
        acc[...] = added if c == 0 else acc[...] + added
    for rows, near_ref in placed_rows(near_refs):
        near_ref[...] = acc[rows, :].astype(BF16)


def own_grad_kernel(chunks, slots_ref, w_dst_ref, *refs):
    grid_hbm, own_ref, grid_ref, dsum_ref, wide_ref, hot_ref, sems = refs[-7:]
    stores = []
    for c in range(chunks):
        dz_ref, dpre_ref = refs[2 * c : 2 * c + 2]
        edges, points, channels = dpre_ref.shape
        rows = slice(c * points, (c + 1) * points)
        for part in strips(points):
            d_sum = sum(dpre_ref[k, part, :].astype(F32) for k in range(edges))
            dsum_ref[part, :] = d_sum.astype(BF16)
        wide_ref[...] = mm_t(dsum_ref[...], w_dst_ref[...])
        for part in strips(points):
            d_grid = dz_ref[part, :].astype(F32) + wide_ref[part, :]
            grid_ref[rows.start + part.start : rows.start + part.stop, :] = d_grid.astype(BF16)
        stores.append(pltpu.make_async_copy(grid_ref.at[rows], grid_hbm.at[rows], sems.at[c]))
        stores[-1].start()
        fill_rows(hot_ref.at[c], slots_ref[:, rows], 0)
        added = mm(hot_ref[c], dpre_ref[...].reshape(edges * points, channels))
        own_ref[...] = added if c == 0 else own_ref[...] + added
    for store in stores:
        store.wait()


def merge_kernel(send_ref, own_ref, w_src_ref, *refs):
    *near_refs, base_ref, hot_ref, near_ref, near_hot = refs
    join(near_refs, near_ref)
    near, far = near_far(send_ref[0:1, :], send_ref[1:2, :])
    fill_rows(near_hot, near, 0)
    total = own_ref[...] + mm(near_hot[...], near_ref[...])
    base_ref[...] = mm_t(total.astype(BF16), w_src_ref[...])
    fill_rows(hot_ref, far, 0)


def mesh_kernel(hot_ref, base_ref, w_src_ref, *refs):
    *far_refs, mesh_hbm, rows_ref, out_ref, sems = refs
    owned = base_ref.shape[0]
    size = far_refs[0].shape[0]
    for i, far_ref in enumerate(far_refs):
        rows_ref[i * size : (i + 1) * size, :] = mm_t(far_ref[...], w_src_ref[...]).astype(BF16)
    stores = []
    for i, part in enumerate(pieces(owned, owned // 4)):
        out = base_ref[part, :] + mm(hot_ref[part, :], rows_ref[...])
        out_ref[part, :] = out.astype(BF16)
        stores.append(pltpu.make_async_copy(out_ref.at[part], mesh_hbm.at[part], sems.at[i]))
        stores[-1].start()
    for store in stores:
        store.wait()


def per_device(
    grid_latent,
    mesh_latent,
    edge_attr,
    neighbours,
    send_rows,
    target,
    field_weight,
    w_src,
    w_dst,
    w_edge,
    w_msg,
    ln_gain,
    w_out,
):
    grid_rows = grid_latent[0]
    mesh_rows = mesh_latent[0]
    points, channels = grid_rows.shape
    owned = mesh_rows.shape[0]
    halo = send_rows.shape[1]
    edges = neighbours.shape[1]
    feats = w_edge.shape[0]
    lanes = 128
    fields = -(-w_out.shape[1] // lanes) * lanes
    sent = -(-w_out.shape[1] // 16) * 16
    block = min(points, 512)
    sds = jax.ShapeDtypeStruct
    members = lax.axis_size("member")
    bands = lax.axis_size("band")
    near_swap = swap(range(0, bands - 1, 2))
    far_swap = swap(range(1, bands - 1, 2))
    vmem, far_memory = pltpu.VMEM, pltpu.HBM
    slots = neighbours.T
    gain = ln_gain[None, :]
    w_out = w_out.T
    weight = field_weight[None, :]

    far_shapes = [sds((halo, channels), BF16)]
    near_shapes = [sds((halo // 2, channels), BF16)] * 2
    held = [grid_rows, w_dst]
    *far, mesh_rows, w_src, grid_rows, w_dst = call(
        functools.partial(far_kernel, len(held)),
        [far_memory] * (3 + len(held)),
        [vmem] * (3 + len(held)),
        far_shapes + [sds(array.shape, BF16) for array in (mesh_rows, w_src, *held)],
        2 * owned * channels * halo,
        2 * owned * channels,
        [
            vmem((2, halo), jnp.int32),
            pltpu.SemaphoreType.DMA((4 + len(held),)),
        ],
    )(*map(hbm, (mesh_rows, w_src, send_rows, *held)))
    far = [lax.ppermute(piece, "band", far_swap) for piece in far]

    src, *near = call(
        near_kernel,
        [vmem] * 3,
        [vmem] * (1 + len(near_shapes)),
        [sds((owned, channels), BF16), *near_shapes],
        *IN_SHADOW,
    )(mesh_rows, w_src, send_rows)
    near = [lax.ppermute(piece, "band", near_swap) for piece in near]

    chunks = 2
    part = points // chunks
    pre, columns, rows = call(
        functools.partial(own_kernel, block),
        [vmem] * (6 + len(near)),
        [vmem] * 3,
        [
            sds((edges, points, channels), BF16),
            sds((edges, points, halo), BF16),
            sds((chunks, halo, edges * part), BF16),
        ],
        *IN_SHADOW,
        [
            vmem((points // block, block, channels), F32),
            vmem((edges, lanes, channels), BF16),
            vmem((feats * edges, points), F32),
            vmem((halo, channels), BF16),
        ],
    )(slots, src, grid_rows, w_dst, edge_attr, w_edge, *near)

    ahead = []
    for c in range(chunks):
        pred, pred_bf, sg, zhat, rstd = call(
            functools.partial(forward_kernel, c * part, block, fields),
            [vmem] * (6 + len(far)),
            [vmem] * 5,
            [
                sds((fields, part), F32),
                sds((sent, part), BF16),
                sds((edges, part, channels), BF16),
                sds((part, channels), BF16),
                sds((part, lanes), F32),
            ],
            2 * part * channels * (edges * halo + channels),
            part * channels * edges * 4,
        )(columns, pre, grid_rows, w_msg, gain, w_out, *far)
        if members == 2:
            others = lax.ppermute(pred_bf, "member", [(0, 1), (1, 0)])[None]
        else:
            others = lax.all_gather(pred_bf[None], "member", axis=0, tiled=True)
        ahead.append((pred, others, sg, zhat, rstd))

    coeff = ALPHA / (members - 1) + (1.0 - ALPHA) / members
    far = []
    d_zs, d_pres = [], []
    for c, (pred, others, sg, zhat, rstd) in enumerate(ahead):
        rim_shapes = far_shapes if c == chunks - 1 else [sds((halo, channels), F32)]
        d_z, d_pre, *far = call(
            functools.partial(backward_kernel, c, block, coeff, len(far)),
            [vmem] * (11 + len(far)),
            [vmem] * (2 + len(rim_shapes)),
            [sds((part, channels), BF16), sds((edges, part, channels), BF16), *rim_shapes],
            2 * part * channels * (edges * halo + channels),
            part * channels * edges * 4,
            [
                vmem((part, fields), BF16),
                vmem((part, channels), F32),
            ],
        )(rows, pred, others, target, weight, w_out, gain, zhat, rstd, w_msg, sg, *far)
        d_zs.append(d_z)
        d_pres.append(d_pre)
    far = [lax.ppermute(piece, "band", far_swap) for piece in far]

    near = call(
        functools.partial(rim_kernel, owned, chunks),
        [vmem] * (1 + chunks),
        [vmem] * len(near_shapes),
        near_shapes,
        *IN_SHADOW,
        [vmem((halo, channels), F32), vmem((chunks, halo, edges * part), BF16)],
    )(slots, *d_pres)
    near = [lax.ppermute(piece, "band", near_swap) for piece in near]

    d_grid, own = call(
        functools.partial(own_grad_kernel, chunks),
        [vmem] * (2 + 2 * chunks),
        [far_memory, vmem],
        [sds((points, channels), BF16), sds((owned, channels), F32)],
        *IN_SHADOW,
        [
            vmem((points, channels), BF16),
            vmem((part, channels), BF16),
            vmem((part, channels), F32),
            vmem((chunks, owned, edges * part), BF16),
            pltpu.SemaphoreType.DMA((chunks,)),
        ],
    )(slots, w_dst, *[ref for pair in zip(d_zs, d_pres) for ref in pair])

    base, far_hot = call(
        merge_kernel,
        [vmem] * (3 + len(near)),
        [vmem] * 2,
        [sds((owned, channels), F32), sds((owned, halo), BF16)],
        *IN_SHADOW,
        [vmem((halo, channels), BF16), vmem((owned, halo), BF16)],
    )(send_rows, own, w_src, *near)

    [d_mesh] = call(
        mesh_kernel,
        [vmem] * (3 + len(far)),
        [far_memory],
        [sds((owned, channels), BF16)],
        2 * owned * channels * (channels + halo),
        owned * channels * 8,
        [
            vmem((halo, channels), BF16),
            vmem((owned, channels), BF16),
            pltpu.SemaphoreType.DMA((4,)),
        ],
    )(far_hot, base, w_src, *far)
    return (d_grid[None], d_mesh[None])


def solution(mesh):
    placed = (
        P("member", "band", None),
        P("member", "band", None),
        P(None, None, "band"),
        P("band", None),
        P("band", None),
        P(None, "band"),
        P(),
        P(),
        P(),
        P(),
        P(),
        P(),
        P(),
    )
    return jax.shard_map(
        per_device,
        mesh=mesh,
        in_specs=placed,
        out_specs=(P("member", "band", None), P("member", "band", None)),
        check_vma=False,
    )
```

profile of v0, /device:TPU:1, one launch (start us, length us, event | category | flops | bytes accessed | tf_op | source)
XLA Modules:
  0.0 50.8 jit_solution(15374461665581026696)
XLA Ops:
  0.7 2.4 %shard_map.140 = (bf16[512,512]{1,0:T(8,128)(2,1)S(1)}, bf16[1024,512]{1,0:T(8,128)(2,1)S(1)}, bf16[512,512]{1,0:T(8,128)(2,1)S(1)}, bf16[1024,512]{1,0:T(8,128)(2,1)S(1)}, bf16[512,512]{1,0:T(8,128)(2,1)S(1)}) custom-call(bf16[1024,512]{1,0:T(8,128)(2,1)} %bitcast.26, bf16[512,512]{1,0:T(8,128)(2,1)} %w_src_hbm.1, s32[2,512]{1,0:T(2,128)} %send_ref.3, ...), custom_call_target="tpu_custom_call" | custom-call | flops 536870912 | bytes 1048576 | tf_op jit(solution)/shard_map/pallas_call | solution.py:403
  3.1 4.5 %collective-permute-start.2 = (bf16[512,512]{1,0:T(8,128)(2,1)S(1)}, bf16[512,512]{1,0:T(8,128)(2,1)S(1)}, u32[]{:S(2)}, u32[]{:S(2)}) collective-permute-start(bf16[512,512]{1,0:T(8,128)(2,1)S(1)} %get-tuple-element.45), channel_id=1, source_target_pairs={{2,4},{4,2},{6,8},{8,6},{10,12},{12,10},{14,16},{16,14},{18,20},{2... | collective-permute-start | bytes 1572872 | tf_op jit(solution)/shard_map/ppermute | solution.py:415
  7.7 1.2 %shard_map.141 = (bf16[1024,512]{1,0:T(8,128)(2,1)S(1)}, bf16[256,512]{1,0:T(8,128)(2,1)S(1)}, bf16[256,512]{1,0:T(8,128)(2,1)S(1)}) custom-call(bf16[1024,512]{1,0:T(8,128)(2,1)S(1)} %get-tuple-element.36.mesh_ref, bf16[512,512]{1,0:T(8,128)(2,1)S(1)} %get-tuple-element.37.w_src_ref, s32[2,512]{1,0:T(2,128)S(1)} %copy-done.4), custom_call_target="tpu_custom_call" | custom-call | flops 1 | bytes 1 | tf_op jit(solution)/shard_map/pallas_call | solution.py:417
  9.0 0.1 collective-permute-start
  9.0 0.5 collective-permute-start.1
  9.5 1.0 %collective-permute-done.refs_0_ = bf16[256,512]{1,0:T(8,128)(2,1)S(1)} collective-permute-done((bf16[256,512]{1,0:T(8,128)(2,1)S(1)}, bf16[256,512]{1,0:T(8,128)(2,1)S(1)}, u32[]{:S(2)}, u32[]{:S(2)}) %collective-permute-start) | collective-permute-done | bytes 262176 | tf_op jit(solution)/shard_map/ppermute | solution.py:424
  10.6 0.4 collective-permute-done.1.refs_1_
  11.0 8.9 %shard_map.142 = (bf16[4,1024,512]{2,1,0:T(8,128)(2,1)S(1)}, bf16[4,1024,512]{2,1,0:T(8,128)(2,1)S(1)}, bf16[2,512,2048]{2,1,0:T(8,128)(2,1)S(1)}) custom-call(s32[4,1024]{1,0:T(4,128)S(1)} %bitcast.14, bf16[1024,512]{1,0:T(8,128)(2,1)S(1)} %get-tuple-element.38.src_ref, bf16[1024,512]{1,0:T(8,128)(2,1)S(1)} %get-tuple-element.39.grid_ref, ...), custom_call_target="tpu_custom_call" | custom-call | flops 1 | bytes 1 | tf_op jit(solution)/shard_map/pallas_call | solution.py:428
  19.9 2.3 %shard_map.143 = (f32[128,512]{1,0:T(8,128)S(1)}, bf16[112,512]{1,0:T(8,128)(2,1)S(1)}, bf16[4,512,512]{2,1,0:T(8,128)(2,1)S(1)}, bf16[512,512]{1,0:T(8,128)(2,1)S(1)}, f32[512,128]{1,0:T(8,128)S(1)}) custom-call(bf16[4,1024,512]{2,1,0:T(8,128)(2,1)S(1)} %get-tuple-element.43.columns_ref, bf16[4,1024,512]{2,1,0:T(8,128)(2,1)S(1)} %get-tuple-element.44.pre_ref, ...), custom_call_target="tpu_custom_call" | custom-call | flops 1342177280 | bytes 4194304 | tf_op jit(solution)/shard_map/pallas_call | solution.py:448
  22.2 1.3 %collective-permute-start.3 = (bf16[112,512]{1,0:T(8,128)(2,1)S(1)}, bf16[112,512]{1,0:T(8,128)(2,1)S(1)}, u32[]{:S(2)}, u32[]{:S(2)}) collective-permute-start(bf16[112,512]{1,0:T(8,128)(2,1)S(1)} %get-tuple-element.47), channel_id=1, source_target_pairs={{0,1},{1,0},{2,3},{3,2},{4,5},{5,4},{6,7},{7,6},{8,9},{9,8},{10,11... | collective-permute-start | bytes 344072 | tf_op jit(solution)/shard_map/ppermute | solution.py:463
  23.5 2.3 %shard_map.145 = (f32[128,512]{1,0:T(8,128)S(1)}, bf16[112,512]{1,0:T(8,128)(2,1)S(1)}, bf16[4,512,512]{2,1,0:T(8,128)(2,1)S(1)}, bf16[512,512]{1,0:T(8,128)(2,1)S(1)}, f32[512,128]{1,0:T(8,128)S(1)}) custom-call(bf16[4,1024,512]{2,1,0:T(8,128)(2,1)S(1)} %get-tuple-element.43.columns_ref, bf16[4,1024,512]{2,1,0:T(8,128)(2,1)S(1)} %get-tuple-element.44.pre_ref, ...), custom_call_target="tpu_custom_call" | custom-call | flops 1342177280 | bytes 4194304 | tf_op jit(solution)/shard_map/pallas_call | solution.py:448
  25.8 0.3 collective-permute-start.4
  26.1 0.8 %collective-permute-done.3 = bf16[112,512]{1,0:T(8,128)(2,1)S(1)} collective-permute-done((bf16[112,512]{1,0:T(8,128)(2,1)S(1)}, bf16[112,512]{1,0:T(8,128)(2,1)S(1)}, u32[]{:S(2)}, u32[]{:S(2)}) %collective-permute-start.3) | collective-permute-done | bytes 114720 | tf_op jit(solution)/shard_map/ppermute | solution.py:463
  26.9 2.5 %shard_map.144 = (bf16[512,512]{1,0:T(8,128)(2,1)S(1)}, bf16[4,512,512]{2,1,0:T(8,128)(2,1)S(1)}, f32[512,512]{1,0:T(8,128)S(1)}) custom-call(bf16[2,512,2048]{2,1,0:T(8,128)(2,1)S(1)} %get-tuple-element.42.hot_ref, f32[128,512]{1,0:T(8,128)S(1)} %get-tuple-element.46.pred_ref, bf16[1,112,512]{2,1,0:T(8,128)(2,1)S(1)} %bitcast.18, ...), custom_call_target="tpu_custom_call" | custom-call | flops 1342177280 | bytes 4194304 | tf_op jit(solution)/shard_map/pallas_call | solution.py:473
  29.4 0.8 %collective-permute-done.4 = bf16[112,512]{1,0:T(8,128)(2,1)S(1)} collective-permute-done((bf16[112,512]{1,0:T(8,128)(2,1)S(1)}, bf16[112,512]{1,0:T(8,128)(2,1)S(1)}, u32[]{:S(2)}, u32[]{:S(2)}) %collective-permute-start.4) | collective-permute-done | bytes 114720 | tf_op jit(solution)/shard_map/ppermute | solution.py:463
  30.2 2.3 %shard_map.146 = (bf16[512,512]{1,0:T(8,128)(2,1)S(1)}, bf16[4,512,512]{2,1,0:T(8,128)(2,1)S(1)}, bf16[512,512]{1,0:T(8,128)(2,1)S(1)}) custom-call(bf16[2,512,2048]{2,1,0:T(8,128)(2,1)S(1)} %get-tuple-element.42.hot_ref, f32[128,512]{1,0:T(8,128)S(1)} %get-tuple-element.53.pred_ref, bf16[1,112,512]{2,1,0:T(8,128)(2,1)S(1)} %bitcast.17, ...), custom_call_target="tpu_custom_call" | custom-call | flops 1342177280 | bytes 4194304 | tf_op jit(solution)/shard_map/pallas_call | solution.py:473
  32.5 4.6 %collective-permute-start.7 = (bf16[512,512]{1,0:T(8,128)(2,1)S(1)}, bf16[512,512]{1,0:T(8,128)(2,1)S(1)}, u32[]{:S(2)}, u32[]{:S(2)}) collective-permute-start(bf16[512,512]{1,0:T(8,128)(2,1)S(1)} %get-tuple-element.67), channel_id=1, source_target_pairs={{2,4},{4,2},{6,8},{8,6},{10,12},{12,10},{14,16},{16,14},{18,20},{2... | collective-permute-start | bytes 1572872 | tf_op jit(solution)/shard_map/ppermute | solution.py:487
  37.1 2.3 %shard_map.148 = (bf16[256,512]{1,0:T(8,128)(2,1)S(1)}, bf16[256,512]{1,0:T(8,128)(2,1)S(1)}) custom-call(s32[4,1024]{1,0:T(4,128)S(1)} %bitcast.15, bf16[4,512,512]{2,1,0:T(8,128)(2,1)S(1)} %get-tuple-element.52.refs_1_.refs_0_, bf16[4,512,512]{2,1,0:T(8,128)(2,1)S(1)} %get-tuple-element.60.refs_3_.refs_1_), custom_call_target="tpu_custom_call" | custom-call | flops 1 | bytes 1 | tf_op jit(solution)/shard_map/pallas_call | solution.py:489
  39.4 0.1 collective-permute-start.5
  39.5 0.5 collective-permute-start.6
  40.0 5.1 %shard_map.147 = (bf16[1024,512]{1,0:T(8,128)(2,1)}, f32[1024,512]{1,0:T(8,128)S(1)}) custom-call(s32[4,1024]{1,0:T(4,128)S(1)} %bitcast.16, bf16[512,512]{1,0:T(8,128)(2,1)S(1)} %get-tuple-element.35.w_dst_ref, bf16[512,512]{1,0:T(8,128)(2,1)S(1)} %get-tuple-element.51.refs_0_, bf16[4,512,512]{2,1,0:T(8,128)(2,1)S(1)} %get-tuple-element.52.refs_1_.refs_0_, ...), custom_call_target="tpu_custom_call" | custom-call | flops 1 | bytes 1 | tf_op jit(solution)/shard_map/pallas_call | solution.py:499
  45.2 1.4 %shard_map.149 = (f32[1024,512]{1,0:T(8,128)S(1)}, bf16[1024,512]{1,0:T(8,128)(2,1)S(1)}) custom-call(s32[2,512]{1,0:T(2,128)S(1)} %copy-done.4, f32[1024,512]{1,0:T(8,128)S(1)} %get-tuple-element.62.own_ref, bf16[512,512]{1,0:T(8,128)(2,1)S(1)} %get-tuple-element.37.w_src_ref, bf16[256,512]{1,0:T(8,128)(2,1)S(1)} %collective-permute-done.5.refs_0_, ...), custom_call_target="tpu_custom_call" | custom-call | flops 1 | bytes 1 | tf_op jit(solution)/shard_map/pallas_call | solution.py:514
  46.5 2.3 %collective-permute-done.7.refs_0_ = bf16[512,512]{1,0:T(8,128)(2,1)S(1)} collective-permute-done((bf16[512,512]{1,0:T(8,128)(2,1)S(1)}, bf16[512,512]{1,0:T(8,128)(2,1)S(1)}, u32[]{:S(2)}, u32[]{:S(2)}) %collective-permute-start.7) | collective-permute-done | bytes 524320 | tf_op jit(solution)/shard_map/ppermute | solution.py:487
  48.8 1.8 %shard_map.150 = bf16[1024,512]{1,0:T(8,128)(2,1)} custom-call(bf16[1024,512]{1,0:T(8,128)(2,1)S(1)} %get-tuple-element.65.hot_ref, f32[1024,512]{1,0:T(8,128)S(1)} %get-tuple-element.66.base_ref, bf16[512,512]{1,0:T(8,128)(2,1)S(1)} %get-tuple-element.37.w_src_ref, bf16[512,512]{1,0:T(8,128)(2,1)S(1)} %collective-permute-done.7.refs_0_), custom_call_target="tpu_custom_call" | custom-call | flops 1073741824 | bytes 4194304 | tf_op jit(solution)/shard_map/pallas_call | solution.py:523
  (21 shorter events, 0.1 us)
Async XLA Ops:
  0.6 7.0 %copy-start.4 = (s32[2,512]{1,0:T(2,128)S(1)}, s32[2,512]{1,0:T(2,128)}, u32[]{:S(2)}) copy-start(s32[2,512]{1,0:T(2,128)} %send_ref.3) | copy-start | bytes 12292
  0.6 10.3 %copy-start.3 = (s32[1024,4]{0,1:T(4,128)S(1)}, s32[1024,4]{0,1:T(4,128)}, u32[]{:S(2)}) copy-start(s32[1024,4]{0,1:T(4,128)} %param.16) | copy-start | bytes 49156
  0.7 10.3 %copy-start.5 = (bf16[4,4,1024]{2,1,0:T(4,128)(2,1)S(1)}, bf16[4,4,1024]{2,1,0:T(4,128)(2,1)}, u32[]{:S(2)}) copy-start(bf16[4,4,1024]{2,1,0:T(4,128)(2,1)} %attr_ref.1) | copy-start | bytes 98308
  0.7 10.3 %copy-start.7 = (bf16[4,512]{1,0:T(4,128)(2,1)S(1)}, bf16[4,512]{1,0:T(4,128)(2,1)}, u32[]{:S(2)}) copy-start(bf16[4,512]{1,0:T(4,128)(2,1)} %w_edge_ref.1) | copy-start | bytes 12292
  3.1 16.8 %collective-permute-start.2 = (bf16[512,512]{1,0:T(8,128)(2,1)S(1)}, bf16[512,512]{1,0:T(8,128)(2,1)S(1)}, u32[]{:S(2)}, u32[]{:S(2)}) collective-permute-start(bf16[512,512]{1,0:T(8,128)(2,1)S(1)} %get-tuple-element.45), channel_id=1, source_target_pairs={{2,4},{4,2},{6,8},{8,6},{10,12},{12,10},{14,16},{16,14},{18,20},{2... | collective-permute-start | bytes 1572872 | tf_op jit(solution)/shard_map/ppermute | solution.py:415
  7.7 12.2 %copy-start = (bf16[512,512]{1,0:T(8,128)(2,1)S(1)}, bf16[512,512]{1,0:T(8,128)(2,1)}, u32[]{:S(2)}) copy-start(bf16[512,512]{1,0:T(8,128)(2,1)} %w_msg_ref.7) | copy-start | bytes 1572868
  7.7 12.2 %copy-start.1 = (bf16[512,100]{0,1:T(8,128)(2,1)S(1)}, bf16[512,100]{0,1:T(8,128)(2,1)}, u32[]{:S(2)}) copy-start(bf16[512,100]{0,1:T(8,128)(2,1)} %param.25) | copy-start | bytes 307204
  7.7 12.2 %copy-start.6 = (f32[512]{0:T(512)S(1)}, f32[512]{0:T(512)}, u32[]{:S(2)}) copy-start(f32[512]{0:T(512)} %param.24) | copy-start | bytes 6148
  9.0 1.6 %collective-permute-start = (bf16[256,512]{1,0:T(8,128)(2,1)S(1)}, bf16[256,512]{1,0:T(8,128)(2,1)S(1)}, u32[]{:S(2)}, u32[]{:S(2)}) collective-permute-start(bf16[256,512]{1,0:T(8,128)(2,1)S(1)} %get-tuple-element.40), channel_id=1, source_target_pairs={{0,2},{2,0},{4,6},{6,4},{8,10},{10,8},{12,14},{14,12},{16,18},{18,... | collective-permute-start | bytes 786440 | tf_op jit(solution)/shard_map/ppermute | solution.py:424
  9.0 1.9 %collective-permute-start.1 = (bf16[256,512]{1,0:T(8,128)(2,1)S(1)}, bf16[256,512]{1,0:T(8,128)(2,1)S(1)}, u32[]{:S(2)}, u32[]{:S(2)}) collective-permute-start(bf16[256,512]{1,0:T(8,128)(2,1)S(1)} %get-tuple-element.41), channel_id=1, source_target_pairs={{0,2},{2,0},{4,6},{6,4},{8,10},{10,8},{12,14},{14,12},{16,18},{18,... | collective-permute-start | bytes 786440 | tf_op jit(solution)/shard_map/ppermute | solution.py:424
  22.2 4.7 %copy-start.2 = (f32[100,1024]{1,0:T(8,128)S(1)}, f32[100,1024]{1,0:T(8,128)}, u32[]{:S(2)}) copy-start(f32[100,1024]{1,0:T(8,128)} %target_ref.3) | copy-start | bytes 1228804
  22.2 4.7 %copy-start.8 = (f32[100]{0:T(128)S(1)}, f32[100]{0:T(128)}, u32[]{:S(2)}) copy-start(f32[100]{0:T(128)} %param.19) | copy-start | bytes 1204
  22.2 4.7 %collective-permute-start.3 = (bf16[112,512]{1,0:T(8,128)(2,1)S(1)}, bf16[112,512]{1,0:T(8,128)(2,1)S(1)}, u32[]{:S(2)}, u32[]{:S(2)}) collective-permute-start(bf16[112,512]{1,0:T(8,128)(2,1)S(1)} %get-tuple-element.47), channel_id=1, source_target_pairs={{0,1},{1,0},{2,3},{3,2},{4,5},{5,4},{6,7},{7,6},{8,9},{9,8},{10,11... | collective-permute-start | bytes 344072 | tf_op jit(solution)/shard_map/ppermute | solution.py:463
  25.8 4.4 %collective-permute-start.4 = (bf16[112,512]{1,0:T(8,128)(2,1)S(1)}, bf16[112,512]{1,0:T(8,128)(2,1)S(1)}, u32[]{:S(2)}, u32[]{:S(2)}) collective-permute-start(bf16[112,512]{1,0:T(8,128)(2,1)S(1)} %get-tuple-element.54), channel_id=1, source_target_pairs={{0,1},{1,0},{2,3},{3,2},{4,5},{5,4},{6,7},{7,6},{8,9},{9,8},{10,11... | collective-permute-start | bytes 344072 | tf_op jit(solution)/shard_map/ppermute | solution.py:463
  32.5 16.3 %collective-permute-start.7 = (bf16[512,512]{1,0:T(8,128)(2,1)S(1)}, bf16[512,512]{1,0:T(8,128)(2,1)S(1)}, u32[]{:S(2)}, u32[]{:S(2)}) collective-permute-start(bf16[512,512]{1,0:T(8,128)(2,1)S(1)} %get-tuple-element.67), channel_id=1, source_target_pairs={{2,4},{4,2},{6,8},{8,6},{10,12},{12,10},{14,16},{16,14},{18,20},{2... | collective-permute-start | bytes 1572872 | tf_op jit(solution)/shard_map/ppermute | solution.py:487
  39.4 5.7 %collective-permute-start.5 = (bf16[256,512]{1,0:T(8,128)(2,1)S(1)}, bf16[256,512]{1,0:T(8,128)(2,1)S(1)}, u32[]{:S(2)}, u32[]{:S(2)}) collective-permute-start(bf16[256,512]{1,0:T(8,128)(2,1)S(1)} %get-tuple-element.63), channel_id=1, source_target_pairs={{0,2},{2,0},{4,6},{6,4},{8,10},{10,8},{12,14},{14,12},{16,18},{18,... | collective-permute-start | bytes 786440 | tf_op jit(solution)/shard_map/ppermute | solution.py:497
  39.5 5.6 %collective-permute-start.6 = (bf16[256,512]{1,0:T(8,128)(2,1)S(1)}, bf16[256,512]{1,0:T(8,128)(2,1)S(1)}, u32[]{:S(2)}, u32[]{:S(2)}) collective-permute-start(bf16[256,512]{1,0:T(8,128)(2,1)S(1)} %get-tuple-element.64), channel_id=1, source_target_pairs={{0,2},{2,0},{4,6},{6,4},{8,10},{10,8},{12,14},{14,12},{16,18},{18,... | collective-permute-start | bytes 786440 | tf_op jit(solution)/shard_map/ppermute | solution.py:497
where the time goes:
time: 51 us; the launch traced here: 50.8 us
  Pallas kernels  32.6 us (64%)
  starting transfers between devices  11.9 us (23%)
  waiting for transfers between devices  5.26 us (10%)
  between operations  1.03 us (2%)
    ppermute x2, starting transfers between devices, per_device(): far = [lax.ppermute(piece, 'band', far_swap) for piece in far]  9.18 us
    pallas_call x1, Pallas kernels, per_device(): call(functools.partial(own_kernel, block), [vmem] * (6 + len(near)), [vme...  8.92 us
    pallas_call x1, Pallas kernels, per_device(): call(functools.partial(own_grad_kernel, chunks), [vmem] * (2 + 2 * chunks...  5.12 us
    pallas_call x2, Pallas kernels, per_device(): call(functools.partial(backward_kernel, c, block, coeff, len(far)), [vmem...  4.75 us
    pallas_call x2, Pallas kernels, per_device(): call(functools.partial(forward_kernel, c * part, block, fields), [vmem] *...  4.56 us
    pallas_call x1, Pallas kernels, per_device(): call(functools.partial(far_kernel, len(held)), [far_memory] * (3 + len(he...  2.44 us
    pallas_call x1, Pallas kernels, per_device(): call(functools.partial(rim_kernel, owned, chunks), [vmem] * (1 + chunks),...  2.32 us
    ppermute x2, waiting for transfers between devices, per_device(): far = [lax.ppermute(piece, 'band', far_swap) for piece in far]  2.27 us
  transfers between devices with their start and end apart: 8, of which 5 were waited for; matrix products, arithmetic and copies ran while one was open for 0% of the time, Pallas kernels for 47%

commit v1 on v0

--- a/solution.py
+++ b/solution.py
@@ -152,17 +152,22 @@
         near_ref[...] = rows[part, :]
 
 
-def own_kernel(
-    block,
-    slots_ref,
-    src_ref,
-    grid_ref,
-    w_dst_ref,
-    attr_ref,
-    w_edge_ref,
-    *refs,
-):
-    *near_refs, pre_ref, columns_ref, rows_ref, dst_ref, embed_ref, attr_f32, near_ref = refs
+def ready_kernel(owned, slots_ref, grid_ref, w_dst_ref, dst_ref, columns_ref, rows_ref):
+    dst_ref[...] = mm(grid_ref[...], w_dst_ref[...])
+    edges, _, halo = columns_ref.shape
+    chunks, _, width = rows_ref.shape
+    far = rim_bases(owned, halo)[1]
+    part = width // edges
+    for c in range(chunks):
+        points = slice(c * part, (c + 1) * part)
+        for k in range(edges):
+            column = column_of(slots_ref[k : k + 1, points])
+            columns_ref[k, points, :] = column_hot(column, far, halo)
+        fill_rows(rows_ref.at[c], slots_ref[:, points], far)
+
+
+def own_kernel(block, slots_ref, src_ref, dst_ref, attr_ref, w_edge_ref, *refs):
+    *near_refs, pre_ref, embed_ref, attr_f32, near_ref = refs
     join(near_refs, near_ref)
     edges, lanes, channels = embed_ref.shape
     feats = w_edge_ref.shape[0]
@@ -177,21 +182,15 @@
         attr_f32[e * edges : (e + 1) * edges, :] = attr_ref[e].astype(F32)
     owned = src_ref.shape[0]
     halo = near_ref.shape[0]
-    base, far = rim_bases(owned, halo)
-    for at, rows in enumerate(pieces(grid_ref.shape[0], block)):
-        dst_ref[at] = mm(grid_ref[rows, :], w_dst_ref[...])
+    base = rim_bases(owned, halo)[0]
+    for rows in pieces(dst_ref.shape[0], block):
         attr = rows_to(attr_f32[:, rows], lanes).T.astype(BF16)
         for k in range(edges):
             column = column_of(slots_ref[k : k + 1, rows])
             picked = mm(column_hot(column, 0, owned), src_ref[...])
             picked = picked + mm(column_hot(column, base, halo), near_ref[...])
             embed = mm(attr, embed_ref[k])
-            pre_ref[k, rows, :] = (picked + embed + dst_ref[at]).astype(BF16)
-            columns_ref[k, rows, :] = column_hot(column, far, halo)
-    chunks, _, width = rows_ref.shape
-    part = width // edges
-    for c in range(chunks):
-        fill_rows(rows_ref.at[c], slots_ref[:, c * part : (c + 1) * part], far)
+            pre_ref[k, rows, :] = (picked + embed + dst_ref[rows, :]).astype(BF16)
 
 
 def forward_kernel(
@@ -254,7 +253,7 @@
     sg_ref,
     *refs,
 ):
-    prior, (dz_ref, dpre_ref, far_ref, dpred_ref, wide_ref) = refs[:given], refs[given:]
+    prior, (dz_ref, dpre_ref, far_ref) = refs[:given], refs[given:]
     fields = pred_ref.shape[0]
     edges, points, channels = dpre_ref.shape
     first = chunk * points
@@ -264,32 +263,26 @@
     gain = gain_ref[...]
     sent = others_ref.shape[1]
     for rows in pieces(points, block):
-        for part in strips(block, 128):
-            part = slice(rows.start + part.start, rows.start + part.stop)
-            pred = pred_ref[:, part]
-            spread = jnp.zeros((sent, 128), F32)
-            for other in range(others_ref.shape[0]):
-                spread = spread + slope(pred[:sent, :] - others_ref[other, :, part].astype(F32))
-            target = target_ref[:, first + part.start : first + part.stop]
-            d_pred = slope(pred - rows_to(target, fields)) - coeff * rows_to(spread, fields)
-            dpred_ref[part, :] = (weight * d_pred.T).astype(BF16)
-        wide_ref[rows, :] = mm(dpred_ref[rows, :], w_out)
-        for part in strips(block, 32):
-            part = slice(rows.start + part.start, rows.start + part.stop)
-            scaled = wide_ref[part, :] * gain
-            zhat = zhat_ref[part, :].astype(F32)
-            d_z = rstd_ref[part, :1] * (
-                scaled
-                - jnp.mean(scaled, axis=1, keepdims=True)
-                - zhat * jnp.mean(scaled * zhat, axis=1, keepdims=True)
-            )
-            dz_ref[part, :] = d_z.astype(BF16)
-        wide_ref[rows, :] = mm_t(dz_ref[rows, :], w_msg_ref[...])
-        for part in strips(block):
-            part = slice(rows.start + part.start, rows.start + part.stop)
-            d_act = wide_ref[part, :].astype(BF16)
-            for k in range(edges):
-                dpre_ref[k, part, :] = d_act * sg_ref[k, part, :]
+        source = slice(first + rows.start, first + rows.stop)
+        pred = pred_ref[:, rows]
+        spread = jnp.zeros((sent, block), F32)
+        for other in range(others_ref.shape[0]):
+            spread = spread + slope(pred[:sent, :] - others_ref[other, :, rows].astype(F32))
+        d_pred = slope(pred - rows_to(target_ref[:, source], fields))
+        d_pred = d_pred - coeff * rows_to(spread, fields)
+        d_pred = (weight * d_pred.T).astype(BF16)
+        scaled = mm(d_pred, w_out) * gain
+        zhat = zhat_ref[rows, :].astype(F32)
+        d_z = rstd_ref[rows, :1] * (
+            scaled
+            - jnp.mean(scaled, axis=1, keepdims=True)
+            - zhat * jnp.mean(scaled * zhat, axis=1, keepdims=True)
+        )
+        d_zb = d_z.astype(BF16)
+        dz_ref[rows, :] = d_zb
+        d_act = mm_t(d_zb, w_msg_ref[...]).astype(BF16)
+        for k in range(edges):
+            dpre_ref[k, rows, :] = d_act * sg_ref[k, rows, :]
     far = mm(hot_ref[chunk], dpre_ref[...].reshape(edges * points, channels))
     if prior:
         far = far + prior[0][...]
@@ -425,23 +418,30 @@
 
     chunks = 2
     part = points // chunks
-    pre, columns, rows = call(
-        functools.partial(own_kernel, block),
-        [vmem] * (6 + len(near)),
+    dst, columns, rows = call(
+        functools.partial(ready_kernel, owned),
+        [vmem] * 3,
         [vmem] * 3,
         [
-            sds((edges, points, channels), BF16),
+            sds((points, channels), F32),
             sds((edges, points, halo), BF16),
             sds((chunks, halo, edges * part), BF16),
         ],
         *IN_SHADOW,
+    )(slots, grid_rows, w_dst)
+
+    [pre] = call(
+        functools.partial(own_kernel, block),
+        [vmem] * (5 + len(near)),
+        [vmem],
+        [sds((edges, points, channels), BF16)],
+        *IN_SHADOW,
         [
-            vmem((points // block, block, channels), F32),
             vmem((edges, lanes, channels), BF16),
             vmem((feats * edges, points), F32),
             vmem((halo, channels), BF16),
         ],
-    )(slots, src, grid_rows, w_dst, edge_attr, w_edge, *near)
+    )(slots, src, dst, edge_attr, w_edge, *near)
 
     ahead = []
     for c in range(chunks):
@@ -477,10 +477,6 @@
             [sds((part, channels), BF16), sds((edges, part, channels), BF16), *rim_shapes],
             2 * part * channels * (edges * halo + channels),
             part * channels * edges * 4,
-            [
-                vmem((part, fields), BF16),
-                vmem((part, channels), F32),
-            ],
         )(rows, pred, others, target, weight, w_out, gain, zhat, rstd, w_msg, sg, *far)
         d_zs.append(d_z)
         d_pres.append(d_pre)

time: 51 us -> 51.1 us (level); the launches traced: 50.8 us -> 50.3 us
  waiting for transfers between devices: 5.26 us -> 4.32 us
    ppermute x4, waiting for transfers between devices: 1.4 us -> 0.01 us  [per_device(): near = [lax.ppermute(piece, 'band', near_swap) for piece in near]]
    ppermute x2, waiting for transfers between devices: 1.58 us -> 2.3 us  [per_device(): others = lax.ppermute(pred_bf, 'member', [(0, 1), (1, 0)])[None]]
    pallas_call x1 -> x2, Pallas kernels: 8.92 us -> 9.36 us  [the longest x1 7.87 us: per_device(): call(functools.partial(own_kernel, block), [vmem] * (5 + len(near)), [vme...]
  transfers between devices with their start and end apart: 8 -> 8, of which waited for: 5 -> 4; matrix products, arithmetic and copies ran while one was open for 0% -> 0% of each run, Pallas kernels for 47% -> 48%
where the time goes in v1:
time: 51.1 us; the launch traced here: 50.3 us
  Pallas kernels  33 us (65%)
  starting transfers between devices  11.9 us (23%)
  waiting for transfers between devices  4.32 us (8%)
  between operations  1.03 us (2%)
    ppermute x2, starting transfers between devices, per_device(): far = [lax.ppermute(piece, 'band', far_swap) for piece in far]  9.15 us
    pallas_call x1, Pallas kernels, per_device(): call(functools.partial(own_kernel, block), [vmem] * (5 + len(near)), [vme...  7.87 us
    pallas_call x1, Pallas kernels, per_device(): call(functools.partial(own_grad_kernel, chunks), [vmem] * (2 + 2 * chunks...  5.14 us
    pallas_call x2, Pallas kernels, per_device(): call(functools.partial(backward_kernel, c, block, coeff, len(far)), [vmem...  4.74 us
    pallas_call x2, Pallas kernels, per_device(): call(functools.partial(forward_kernel, c * part, block, fields), [vmem] *...  4.54 us
    pallas_call x1, Pallas kernels, per_device(): call(functools.partial(far_kernel, len(held)), [far_memory] * (3 + len(he...  2.43 us
    pallas_call x1, Pallas kernels, per_device(): call(functools.partial(rim_kernel, owned, chunks), [vmem] * (1 + chunks),...  2.32 us
    ppermute x2, waiting for transfers between devices, per_device(): others = lax.ppermute(pred_bf, 'member', [(0, 1), (1, 0)])[None]  2.3 us
  transfers between devices with their start and end apart: 8, of which 4 were waited for; matrix products, arithmetic and copies ran while one was open for 0% of the time, Pallas kernels for 48%

profile of v1, /device:TPU:1, one launch (start us, length us, event | category | flops | bytes accessed | tf_op | source)
XLA Modules:
  0.0 50.3 jit_solution(6413170825656521275)
XLA Ops:
  0.7 2.4 %shard_map.140 = (bf16[512,512]{1,0:T(8,128)(2,1)S(1)}, bf16[1024,512]{1,0:T(8,128)(2,1)S(1)}, bf16[512,512]{1,0:T(8,128)(2,1)S(1)}, bf16[1024,512]{1,0:T(8,128)(2,1)S(1)}, bf16[512,512]{1,0:T(8,128)(2,1)S(1)}) custom-call(bf16[1024,512]{1,0:T(8,128)(2,1)} %bitcast.27, bf16[512,512]{1,0:T(8,128)(2,1)} %w_src_hbm.1, s32[2,512]{1,0:T(2,128)} %send_ref.3, ...), custom_call_target="tpu_custom_call" | custom-call | flops 536870912 | bytes 1048576 | tf_op jit(solution)/shard_map/pallas_call | solution.py:396
  3.1 4.5 %collective-permute-start.2 = (bf16[512,512]{1,0:T(8,128)(2,1)S(1)}, bf16[512,512]{1,0:T(8,128)(2,1)S(1)}, u32[]{:S(2)}, u32[]{:S(2)}) collective-permute-start(bf16[512,512]{1,0:T(8,128)(2,1)S(1)} %get-tuple-element.45), channel_id=1, source_target_pairs={{2,4},{4,2},{6,8},{8,6},{10,12},{12,10},{14,16},{16,14},{18,20},{2... | collective-permute-start | bytes 1572872 | tf_op jit(solution)/shard_map/ppermute | solution.py:408
  7.7 1.2 %shard_map.142 = (bf16[1024,512]{1,0:T(8,128)(2,1)S(1)}, bf16[256,512]{1,0:T(8,128)(2,1)S(1)}, bf16[256,512]{1,0:T(8,128)(2,1)S(1)}) custom-call(bf16[1024,512]{1,0:T(8,128)(2,1)S(1)} %get-tuple-element.39.mesh_ref, bf16[512,512]{1,0:T(8,128)(2,1)S(1)} %get-tuple-element.40.w_src_ref, s32[2,512]{1,0:T(2,128)S(1)} %copy-done.4), custom_call_target="tpu_custom_call" | custom-call | flops 1 | bytes 1 | tf_op jit(solution)/shard_map/pallas_call | solution.py:410
  8.9 0.1 collective-permute-start
  9.0 0.5 collective-permute-start.1
  9.5 1.5 %shard_map.141 = (f32[1024,512]{1,0:T(8,128)S(1)}, bf16[4,1024,512]{2,1,0:T(8,128)(2,1)S(1)}, bf16[2,512,2048]{2,1,0:T(8,128)(2,1)S(1)}) custom-call(s32[4,1024]{1,0:T(4,128)S(1)} %bitcast.14, bf16[1024,512]{1,0:T(8,128)(2,1)S(1)} %get-tuple-element.36.grid_ref, bf16[512,512]{1,0:T(8,128)(2,1)S(1)} %get-tuple-element.35.w_dst_ref), custom_call_target="tpu_custom_call" | custom-call | flops 1 | bytes 1 | tf_op jit(solution)/shard_map/pallas_call | solution.py:421
  11.1 7.9 %shard_map.143.pre_ref = bf16[4,1024,512]{2,1,0:T(8,128)(2,1)S(1)} custom-call(s32[4,1024]{1,0:T(4,128)S(1)} %bitcast.15, bf16[1024,512]{1,0:T(8,128)(2,1)S(1)} %get-tuple-element.41.src_ref, f32[1024,512]{1,0:T(8,128)S(1)} %get-tuple-element.42.dst_ref, bf16[4,4,1024]{2,1,0:T(4,128)(2,1)S(1)} %copy-done.5, bf16[4,512]{1,0:T(4,128)(2,1)S(1)} %copy-done.7, ...), custom_call_target="tpu_custom_call" | custom-call | flops 1 | bytes 1 | tf_op jit(solution)/shard_map/pallas_call | solution.py:433
  18.9 0.4 collective-permute-done.2.far_ref
  19.4 2.3 %shard_map.144 = (f32[128,512]{1,0:T(8,128)S(1)}, bf16[112,512]{1,0:T(8,128)(2,1)S(1)}, bf16[4,512,512]{2,1,0:T(8,128)(2,1)S(1)}, bf16[512,512]{1,0:T(8,128)(2,1)S(1)}, f32[512,128]{1,0:T(8,128)S(1)}) custom-call(bf16[4,1024,512]{2,1,0:T(8,128)(2,1)S(1)} %get-tuple-element.38.columns_ref, bf16[4,1024,512]{2,1,0:T(8,128)(2,1)S(1)} %shard_map.143.pre_ref, ...), custom_call_target="tpu_custom_call" | custom-call | flops 1342177280 | bytes 4194304 | tf_op jit(solution)/shard_map/pallas_call | solution.py:448
  21.7 1.3 %collective-permute-start.3 = (bf16[112,512]{1,0:T(8,128)(2,1)S(1)}, bf16[112,512]{1,0:T(8,128)(2,1)S(1)}, u32[]{:S(2)}, u32[]{:S(2)}) collective-permute-start(bf16[112,512]{1,0:T(8,128)(2,1)S(1)} %get-tuple-element.47), channel_id=1, source_target_pairs={{0,1},{1,0},{2,3},{3,2},{4,5},{5,4},{6,7},{7,6},{8,9},{9,8},{10,11... | collective-permute-start | bytes 344072 | tf_op jit(solution)/shard_map/ppermute | solution.py:463
  23.0 2.3 %shard_map.146 = (f32[128,512]{1,0:T(8,128)S(1)}, bf16[112,512]{1,0:T(8,128)(2,1)S(1)}, bf16[4,512,512]{2,1,0:T(8,128)(2,1)S(1)}, bf16[512,512]{1,0:T(8,128)(2,1)S(1)}, f32[512,128]{1,0:T(8,128)S(1)}) custom-call(bf16[4,1024,512]{2,1,0:T(8,128)(2,1)S(1)} %get-tuple-element.38.columns_ref, bf16[4,1024,512]{2,1,0:T(8,128)(2,1)S(1)} %shard_map.143.pre_ref, ...), custom_call_target="tpu_custom_call" | custom-call | flops 1342177280 | bytes 4194304 | tf_op jit(solution)/shard_map/pallas_call | solution.py:448
  25.3 0.3 collective-permute-start.4
  25.6 1.2 %collective-permute-done.3 = bf16[112,512]{1,0:T(8,128)(2,1)S(1)} collective-permute-done((bf16[112,512]{1,0:T(8,128)(2,1)S(1)}, bf16[112,512]{1,0:T(8,128)(2,1)S(1)}, u32[]{:S(2)}, u32[]{:S(2)}) %collective-permute-start.3) | collective-permute-done | bytes 114720 | tf_op jit(solution)/shard_map/ppermute | solution.py:463
  26.8 2.3 %shard_map.145 = (bf16[512,512]{1,0:T(8,128)(2,1)S(1)}, bf16[4,512,512]{2,1,0:T(8,128)(2,1)S(1)}, f32[512,512]{1,0:T(8,128)S(1)}) custom-call(bf16[2,512,2048]{2,1,0:T(8,128)(2,1)S(1)} %get-tuple-element.37.hot_ref, f32[128,512]{1,0:T(8,128)S(1)} %get-tuple-element.46.pred_ref, bf16[1,112,512]{2,1,0:T(8,128)(2,1)S(1)} %bitcast.19, ...), custom_call_target="tpu_custom_call" | custom-call | flops 1342177280 | bytes 4194304 | tf_op jit(solution)/shard_map/pallas_call | solution.py:473
  29.1 1.1 %collective-permute-done.4 = bf16[112,512]{1,0:T(8,128)(2,1)S(1)} collective-permute-done((bf16[112,512]{1,0:T(8,128)(2,1)S(1)}, bf16[112,512]{1,0:T(8,128)(2,1)S(1)}, u32[]{:S(2)}, u32[]{:S(2)}) %collective-permute-start.4) | collective-permute-done | bytes 114720 | tf_op jit(solution)/shard_map/ppermute | solution.py:463
  30.2 2.5 %shard_map.147 = (bf16[512,512]{1,0:T(8,128)(2,1)S(1)}, bf16[4,512,512]{2,1,0:T(8,128)(2,1)S(1)}, bf16[512,512]{1,0:T(8,128)(2,1)S(1)}) custom-call(bf16[2,512,2048]{2,1,0:T(8,128)(2,1)S(1)} %get-tuple-element.37.hot_ref, f32[128,512]{1,0:T(8,128)S(1)} %get-tuple-element.53.pred_ref, bf16[1,112,512]{2,1,0:T(8,128)(2,1)S(1)} %bitcast.18, ...), custom_call_target="tpu_custom_call" | custom-call | flops 1342177280 | bytes 4194304 | tf_op jit(solution)/shard_map/pallas_call | solution.py:473
  32.6 4.6 %collective-permute-start.7 = (bf16[512,512]{1,0:T(8,128)(2,1)S(1)}, bf16[512,512]{1,0:T(8,128)(2,1)S(1)}, u32[]{:S(2)}, u32[]{:S(2)}) collective-permute-start(bf16[512,512]{1,0:T(8,128)(2,1)S(1)} %get-tuple-element.67), channel_id=1, source_target_pairs={{2,4},{4,2},{6,8},{8,6},{10,12},{12,10},{14,16},{16,14},{18,20},{2... | collective-permute-start | bytes 1572872 | tf_op jit(solution)/shard_map/ppermute | solution.py:483
  37.2 2.3 %shard_map.149 = (bf16[256,512]{1,0:T(8,128)(2,1)S(1)}, bf16[256,512]{1,0:T(8,128)(2,1)S(1)}) custom-call(s32[4,1024]{1,0:T(4,128)S(1)} %bitcast.16, bf16[4,512,512]{2,1,0:T(8,128)(2,1)S(1)} %get-tuple-element.52.refs_1_.refs_0_, bf16[4,512,512]{2,1,0:T(8,128)(2,1)S(1)} %get-tuple-element.60.refs_3_.refs_1_), custom_call_target="tpu_custom_call" | custom-call | flops 1 | bytes 1 | tf_op jit(solution)/shard_map/pallas_call | solution.py:485
  39.6 0.1 collective-permute-start.5
  39.7 0.5 collective-permute-start.6
  40.2 5.1 %shard_map.148 = (bf16[1024,512]{1,0:T(8,128)(2,1)}, f32[1024,512]{1,0:T(8,128)S(1)}) custom-call(s32[4,1024]{1,0:T(4,128)S(1)} %bitcast.17, bf16[512,512]{1,0:T(8,128)(2,1)S(1)} %get-tuple-element.35.w_dst_ref, bf16[512,512]{1,0:T(8,128)(2,1)S(1)} %get-tuple-element.51.refs_0_, bf16[4,512,512]{2,1,0:T(8,128)(2,1)S(1)} %get-tuple-element.52.refs_1_.refs_0_, ...), custom_call_target="tpu_custom_call" | custom-call | flops 1 | bytes 1 | tf_op jit(solution)/shard_map/pallas_call | solution.py:495
  45.3 1.4 %shard_map.150 = (f32[1024,512]{1,0:T(8,128)S(1)}, bf16[1024,512]{1,0:T(8,128)(2,1)S(1)}) custom-call(s32[2,512]{1,0:T(2,128)S(1)} %copy-done.4, f32[1024,512]{1,0:T(8,128)S(1)} %get-tuple-element.62.own_ref, bf16[512,512]{1,0:T(8,128)(2,1)S(1)} %get-tuple-element.40.w_src_ref, bf16[256,512]{1,0:T(8,128)(2,1)S(1)} %collective-permute-done.5.refs_0_, ...), custom_call_target="tpu_custom_call" | custom-call | flops 1 | bytes 1 | tf_op jit(solution)/shard_map/pallas_call | solution.py:510
  46.7 1.6 %collective-permute-done.7.refs_0_ = bf16[512,512]{1,0:T(8,128)(2,1)S(1)} collective-permute-done((bf16[512,512]{1,0:T(8,128)(2,1)S(1)}, bf16[512,512]{1,0:T(8,128)(2,1)S(1)}, u32[]{:S(2)}, u32[]{:S(2)}) %collective-permute-start.7) | collective-permute-done | bytes 524320 | tf_op jit(solution)/shard_map/ppermute | solution.py:483
  48.3 1.8 %shard_map.151 = bf16[1024,512]{1,0:T(8,128)(2,1)} custom-call(bf16[1024,512]{1,0:T(8,128)(2,1)S(1)} %get-tuple-element.65.hot_ref, f32[1024,512]{1,0:T(8,128)S(1)} %get-tuple-element.66.base_ref, bf16[512,512]{1,0:T(8,128)(2,1)S(1)} %get-tuple-element.40.w_src_ref, bf16[512,512]{1,0:T(8,128)(2,1)S(1)} %collective-permute-done.7.refs_0_), custom_call_target="tpu_custom_call" | custom-call | flops 1073741824 | bytes 4194304 | tf_op jit(solution)/shard_map/pallas_call | solution.py:519
  (22 shorter events, 0.1 us)
Async XLA Ops:
  0.6 7.0 %copy-start.4 = (s32[2,512]{1,0:T(2,128)S(1)}, s32[2,512]{1,0:T(2,128)}, u32[]{:S(2)}) copy-start(s32[2,512]{1,0:T(2,128)} %send_ref.3) | copy-start | bytes 12292
  0.6 8.9 %copy-start.3 = (s32[1024,4]{0,1:T(4,128)S(1)}, s32[1024,4]{0,1:T(4,128)}, u32[]{:S(2)}) copy-start(s32[1024,4]{0,1:T(4,128)} %param.16) | copy-start | bytes 49156
  3.1 7.9 %copy-start.5 = (bf16[4,4,1024]{2,1,0:T(4,128)(2,1)S(1)}, bf16[4,4,1024]{2,1,0:T(4,128)(2,1)}, u32[]{:S(2)}) copy-start(bf16[4,4,1024]{2,1,0:T(4,128)(2,1)} %attr_ref.1) | copy-start | bytes 98308
  3.1 7.9 %copy-start.7 = (bf16[4,512]{1,0:T(4,128)(2,1)S(1)}, bf16[4,512]{1,0:T(4,128)(2,1)}, u32[]{:S(2)}) copy-start(bf16[4,512]{1,0:T(4,128)(2,1)} %w_edge_ref.1) | copy-start | bytes 12292
  3.1 16.3 %collective-permute-start.2 = (bf16[512,512]{1,0:T(8,128)(2,1)S(1)}, bf16[512,512]{1,0:T(8,128)(2,1)S(1)}, u32[]{:S(2)}, u32[]{:S(2)}) collective-permute-start(bf16[512,512]{1,0:T(8,128)(2,1)S(1)} %get-tuple-element.45), channel_id=1, source_target_pairs={{2,4},{4,2},{6,8},{8,6},{10,12},{12,10},{14,16},{16,14},{18,20},{2... | collective-permute-start | bytes 1572872 | tf_op jit(solution)/shard_map/ppermute | solution.py:408
  8.9 2.1 %collective-permute-start = (bf16[256,512]{1,0:T(8,128)(2,1)S(1)}, bf16[256,512]{1,0:T(8,128)(2,1)S(1)}, u32[]{:S(2)}, u32[]{:S(2)}) collective-permute-start(bf16[256,512]{1,0:T(8,128)(2,1)S(1)} %get-tuple-element.43), channel_id=1, source_target_pairs={{0,2},{2,0},{4,6},{6,4},{8,10},{10,8},{12,14},{14,12},{16,18},{18,... | collective-permute-start | bytes 786440 | tf_op jit(solution)/shard_map/ppermute | solution.py:417
  9.0 2.0 %collective-permute-start.1 = (bf16[256,512]{1,0:T(8,128)(2,1)S(1)}, bf16[256,512]{1,0:T(8,128)(2,1)S(1)}, u32[]{:S(2)}, u32[]{:S(2)}) collective-permute-start(bf16[256,512]{1,0:T(8,128)(2,1)S(1)} %get-tuple-element.44), channel_id=1, source_target_pairs={{0,2},{2,0},{4,6},{6,4},{8,10},{10,8},{12,14},{14,12},{16,18},{18,... | collective-permute-start | bytes 786440 | tf_op jit(solution)/shard_map/ppermute | solution.py:417
  11.0 8.4 %copy-start = (bf16[512,512]{1,0:T(8,128)(2,1)S(1)}, bf16[512,512]{1,0:T(8,128)(2,1)}, u32[]{:S(2)}) copy-start(bf16[512,512]{1,0:T(8,128)(2,1)} %w_msg_ref.7) | copy-start | bytes 1572868
  11.0 8.3 %copy-start.1 = (bf16[512,100]{0,1:T(8,128)(2,1)S(1)}, bf16[512,100]{0,1:T(8,128)(2,1)}, u32[]{:S(2)}) copy-start(bf16[512,100]{0,1:T(8,128)(2,1)} %param.25) | copy-start | bytes 307204
  11.1 8.3 %copy-start.6 = (f32[512]{0:T(512)S(1)}, f32[512]{0:T(512)}, u32[]{:S(2)}) copy-start(f32[512]{0:T(512)} %param.24) | copy-start | bytes 6148
  21.7 5.1 %copy-start.2 = (f32[100,1024]{1,0:T(8,128)S(1)}, f32[100,1024]{1,0:T(8,128)}, u32[]{:S(2)}) copy-start(f32[100,1024]{1,0:T(8,128)} %target_ref.3) | copy-start | bytes 1228804
  21.7 5.1 %copy-start.8 = (f32[100]{0:T(128)S(1)}, f32[100]{0:T(128)}, u32[]{:S(2)}) copy-start(f32[100]{0:T(128)} %param.19) | copy-start | bytes 1204
  21.7 5.1 %collective-permute-start.3 = (bf16[112,512]{1,0:T(8,128)(2,1)S(1)}, bf16[112,512]{1,0:T(8,128)(2,1)S(1)}, u32[]{:S(2)}, u32[]{:S(2)}) collective-permute-start(bf16[112,512]{1,0:T(8,128)(2,1)S(1)} %get-tuple-element.47), channel_id=1, source_target_pairs={{0,1},{1,0},{2,3},{3,2},{4,5},{5,4},{6,7},{7,6},{8,9},{9,8},{10,11... | collective-permute-start | bytes 344072 | tf_op jit(solution)/shard_map/ppermute | solution.py:463
  25.3 4.9 %collective-permute-start.4 = (bf16[112,512]{1,0:T(8,128)(2,1)S(1)}, bf16[112,512]{1,0:T(8,128)(2,1)S(1)}, u32[]{:S(2)}, u32[]{:S(2)}) collective-permute-start(bf16[112,512]{1,0:T(8,128)(2,1)S(1)} %get-tuple-element.54), channel_id=1, source_target_pairs={{0,1},{1,0},{2,3},{3,2},{4,5},{5,4},{6,7},{7,6},{8,9},{9,8},{10,11... | collective-permute-start | bytes 344072 | tf_op jit(solution)/shard_map/ppermute | solution.py:463
  32.6 15.6 %collective-permute-start.7 = (bf16[512,512]{1,0:T(8,128)(2,1)S(1)}, bf16[512,512]{1,0:T(8,128)(2,1)S(1)}, u32[]{:S(2)}, u32[]{:S(2)}) collective-permute-start(bf16[512,512]{1,0:T(8,128)(2,1)S(1)} %get-tuple-element.67), channel_id=1, source_target_pairs={{2,4},{4,2},{6,8},{8,6},{10,12},{12,10},{14,16},{16,14},{18,20},{2... | collective-permute-start | bytes 1572872 | tf_op jit(solution)/shard_map/ppermute | solution.py:483
  39.6 5.7 %collective-permute-start.5 = (bf16[256,512]{1,0:T(8,128)(2,1)S(1)}, bf16[256,512]{1,0:T(8,128)(2,1)S(1)}, u32[]{:S(2)}, u32[]{:S(2)}) collective-permute-start(bf16[256,512]{1,0:T(8,128)(2,1)S(1)} %get-tuple-element.63), channel_id=1, source_target_pairs={{0,2},{2,0},{4,6},{6,4},{8,10},{10,8},{12,14},{14,12},{16,18},{18,... | collective-permute-start | bytes 786440 | tf_op jit(solution)/shard_map/ppermute | solution.py:493
  39.7 5.7 %collective-permute-start.6 = (bf16[256,512]{1,0:T(8,128)(2,1)S(1)}, bf16[256,512]{1,0:T(8,128)(2,1)S(1)}, u32[]{:S(2)}, u32[]{:S(2)}) collective-permute-start(bf16[256,512]{1,0:T(8,128)(2,1)S(1)} %get-tuple-element.64), channel_id=1, source_target_pairs={{0,2},{2,0},{4,6},{6,4},{8,10},{10,8},{12,14},{14,12},{16,18},{18,... | collective-permute-start | bytes 786440 | tf_op jit(solution)/shard_map/ppermute | solution.py:493

commit v2 on v1

--- a/solution.py
+++ b/solution.py
@@ -152,8 +152,35 @@
         near_ref[...] = rows[part, :]
 
 
-def ready_kernel(owned, slots_ref, grid_ref, w_dst_ref, dst_ref, columns_ref, rows_ref):
+def ready_kernel(
+    owned,
+    slots_ref,
+    grid_ref,
+    w_dst_ref,
+    w_msg_ref,
+    w_src_ref,
+    w_out_ref,
+    target_ref,
+    weight_ref,
+    dst_ref,
+    columns_ref,
+    rows_ref,
+    w_msg_t_ref,
+    w_src_t_ref,
+    w_out_all_ref,
+    target_all_ref,
+    weight_all_ref,
+):
     dst_ref[...] = mm(grid_ref[...], w_dst_ref[...])
+    w_msg_t_ref[...] = w_msg_ref[...].T
+    w_src_t_ref[...] = w_src_ref[...].T
+    fields = target_all_ref.shape[0]
+    w_out_all_ref[...] = rows_to(w_out_ref[...], fields).astype(BF16)
+    target_all_ref[...] = rows_to(target_ref[...], fields)
+    weight = weight_ref[...]
+    weight_all_ref[...] = jnp.concatenate(
+        [weight, jnp.zeros((1, fields - weight.shape[1]), F32)], axis=1
+    )
     edges, _, halo = columns_ref.shape
     chunks, _, width = rows_ref.shape
     far = rim_bases(owned, halo)[1]
@@ -196,7 +223,6 @@
 def forward_kernel(
     first,
     block,
-    fields,
     columns_ref,
     pre_ref,
     grid_ref,
@@ -211,7 +237,6 @@
     rstd_ref,
 ):
     half = BF16(0.5)
-    w_out = rows_to(w_out_ref[...], fields).astype(BF16)
     for rows in pieces(zhat_ref.shape[0], block):
         source = slice(first + rows.start, first + rows.stop)
         acts = []
@@ -228,7 +253,7 @@
         centre = z - jnp.mean(z, axis=1, keepdims=True)
         rstd = lax.rsqrt(jnp.mean(centre * centre, axis=1, keepdims=True) + LN_EPS)
         zhat = centre * rstd
-        pred = mm_t(w_out, (zhat * gain_ref[...]).astype(BF16))
+        pred = mm_t(w_out_ref[...], (zhat * gain_ref[...]).astype(BF16))
         pred_ref[:, rows] = pred
         pred_bf_ref[:, rows] = pred[: pred_bf_ref.shape[0], :].astype(BF16)
         zhat_ref[rows, :] = zhat.astype(BF16)
@@ -249,7 +274,7 @@
     gain_ref,
     zhat_ref,
     rstd_ref,
-    w_msg_ref,
+    w_msg_t_ref,
     sg_ref,
     *refs,
 ):
@@ -257,9 +282,6 @@
     fields = pred_ref.shape[0]
     edges, points, channels = dpre_ref.shape
     first = chunk * points
-    weight = weight_ref[...]
-    weight = jnp.concatenate([weight, jnp.zeros((1, fields - weight.shape[1]), F32)], axis=1)
-    w_out = rows_to(w_out_ref[...], fields).astype(BF16)
     gain = gain_ref[...]
     sent = others_ref.shape[1]
     for rows in pieces(points, block):
@@ -268,10 +290,10 @@
         spread = jnp.zeros((sent, block), F32)
         for other in range(others_ref.shape[0]):
             spread = spread + slope(pred[:sent, :] - others_ref[other, :, rows].astype(F32))
-        d_pred = slope(pred - rows_to(target_ref[:, source], fields))
+        d_pred = slope(pred - target_ref[:, source])
         d_pred = d_pred - coeff * rows_to(spread, fields)
-        d_pred = (weight * d_pred.T).astype(BF16)
-        scaled = mm(d_pred, w_out) * gain
+        d_pred = (weight_ref[...] * d_pred.T).astype(BF16)
+        scaled = mm(d_pred, w_out_ref[...]) * gain
         zhat = zhat_ref[rows, :].astype(F32)
         d_z = rstd_ref[rows, :1] * (
             scaled
@@ -280,7 +302,7 @@
         )
         d_zb = d_z.astype(BF16)
         dz_ref[rows, :] = d_zb
-        d_act = mm_t(d_zb, w_msg_ref[...]).astype(BF16)
+        d_act = mm(d_zb, w_msg_t_ref[...]).astype(BF16)
         for k in range(edges):
             dpre_ref[k, rows, :] = d_act * sg_ref[k, rows, :]
     far = mm(hot_ref[chunk], dpre_ref[...].reshape(edges * points, channels))
@@ -327,22 +349,22 @@
         store.wait()
 
 
-def merge_kernel(send_ref, own_ref, w_src_ref, *refs):
+def merge_kernel(send_ref, own_ref, w_src_t_ref, *refs):
     *near_refs, base_ref, hot_ref, near_ref, near_hot = refs
     join(near_refs, near_ref)
     near, far = near_far(send_ref[0:1, :], send_ref[1:2, :])
     fill_rows(near_hot, near, 0)
     total = own_ref[...] + mm(near_hot[...], near_ref[...])
-    base_ref[...] = mm_t(total.astype(BF16), w_src_ref[...])
+    base_ref[...] = mm(total.astype(BF16), w_src_t_ref[...])
     fill_rows(hot_ref, far, 0)
 
 
-def mesh_kernel(hot_ref, base_ref, w_src_ref, *refs):
+def mesh_kernel(hot_ref, base_ref, w_src_t_ref, *refs):
     *far_refs, mesh_hbm, rows_ref, out_ref, sems = refs
     owned = base_ref.shape[0]
     size = far_refs[0].shape[0]
     for i, far_ref in enumerate(far_refs):
-        rows_ref[i * size : (i + 1) * size, :] = mm_t(far_ref[...], w_src_ref[...]).astype(BF16)
+        rows_ref[i * size : (i + 1) * size, :] = mm(far_ref[...], w_src_t_ref[...]).astype(BF16)
     stores = []
     for i, part in enumerate(pieces(owned, owned // 4)):
         out = base_ref[part, :] + mm(hot_ref[part, :], rows_ref[...])
@@ -392,12 +414,12 @@
 
     far_shapes = [sds((halo, channels), BF16)]
     near_shapes = [sds((halo // 2, channels), BF16)] * 2
-    held = [grid_rows, w_dst]
-    *far, mesh_rows, w_src, grid_rows, w_dst = call(
+    held = [grid_rows, w_dst, w_msg, target]
+    *far, mesh_rows, w_src, grid_rows, w_dst, w_msg, target = call(
         functools.partial(far_kernel, len(held)),
         [far_memory] * (3 + len(held)),
         [vmem] * (3 + len(held)),
-        far_shapes + [sds(array.shape, BF16) for array in (mesh_rows, w_src, *held)],
+        far_shapes + [sds(array.shape, array.dtype) for array in (mesh_rows, w_src, *held)],
         2 * owned * channels * halo,
         2 * owned * channels,
         [
@@ -418,17 +440,22 @@
 
     chunks = 2
     part = points // chunks
-    dst, columns, rows = call(
+    dst, columns, rows, w_msg_t, w_src_t, w_out, target, weight = call(
         functools.partial(ready_kernel, owned),
-        [vmem] * 3,
-        [vmem] * 3,
+        [vmem] * 8,
+        [vmem] * 8,
         [
             sds((points, channels), F32),
             sds((edges, points, halo), BF16),
             sds((chunks, halo, edges * part), BF16),
+            sds(w_msg.shape, BF16),
+            sds(w_src.shape, BF16),
+            sds((fields, channels), BF16),
+            sds((fields, points), F32),
+            sds((1, fields), F32),
         ],
         *IN_SHADOW,
-    )(slots, grid_rows, w_dst)
+    )(slots, grid_rows, w_dst, w_msg, w_src, w_out, target, weight)
 
     [pre] = call(
         functools.partial(own_kernel, block),
@@ -446,7 +473,7 @@
     ahead = []
     for c in range(chunks):
         pred, pred_bf, sg, zhat, rstd = call(
-            functools.partial(forward_kernel, c * part, block, fields),
+            functools.partial(forward_kernel, c * part, block),
             [vmem] * (6 + len(far)),
             [vmem] * 5,
             [
@@ -477,7 +504,7 @@
             [sds((part, channels), BF16), sds((edges, part, channels), BF16), *rim_shapes],
             2 * part * channels * (edges * halo + channels),
             part * channels * edges * 4,
-        )(rows, pred, others, target, weight, w_out, gain, zhat, rstd, w_msg, sg, *far)
+        )(rows, pred, others, target, weight, w_out, gain, zhat, rstd, w_msg_t, sg, *far)
         d_zs.append(d_z)
         d_pres.append(d_pre)
     far = [lax.ppermute(piece, "band", far_swap) for piece in far]
@@ -514,7 +541,7 @@
         [sds((owned, channels), F32), sds((owned, halo), BF16)],
         *IN_SHADOW,
         [vmem((halo, channels), BF16), vmem((owned, halo), BF16)],
-    )(send_rows, own, w_src, *near)
+    )(send_rows, own, w_src_t, *near)
 
     [d_mesh] = call(
         mesh_kernel,
@@ -528,7 +555,7 @@
             vmem((owned, channels), BF16),
             pltpu.SemaphoreType.DMA((4,)),
         ],
-    )(far_hot, base, w_src, *far)
+    )(far_hot, base, w_src_t, *far)
     return (d_grid[None], d_mesh[None])
 
 

time: 51.1 us -> 51.1 us (level)
  no operation moved by 1% of the time
where the time goes in v2:
time: 51.1 us; the launch traced here: 50.6 us
  Pallas kernels  33.2 us (65%)
  starting transfers between devices  12 us (23%)
  waiting for transfers between devices  4.29 us (8%)
  between operations  1.01 us (2%)
    ppermute x2, starting transfers between devices, per_device(): far = [lax.ppermute(piece, 'band', far_swap) for piece in far]  9.29 us
    pallas_call x1, Pallas kernels, per_device(): call(functools.partial(own_kernel, block), [vmem] * (5 + len(near)), [vme...  7.81 us
    pallas_call x1, Pallas kernels, per_device(): call(functools.partial(own_grad_kernel, chunks), [vmem] * (2 + 2 * chunks...  5.14 us
    pallas_call x2, Pallas kernels, per_device(): call(functools.partial(backward_kernel, c, block, coeff, len(far)), [vmem...  4.73 us
    pallas_call x2, Pallas kernels, per_device(): call(functools.partial(forward_kernel, c * part, block), [vmem] * (6 + le...  4.54 us
    pallas_call x1, Pallas kernels, per_device(): call(functools.partial(far_kernel, len(held)), [far_memory] * (3 + len(he...  2.5 us
    pallas_call x1, Pallas kernels, per_device(): call(functools.partial(rim_kernel, owned, chunks), [vmem] * (1 + chunks),...  2.32 us
    ppermute x2, waiting for transfers between devices, per_device(): others = lax.ppermute(pred_bf, 'member', [(0, 1), (1, 0)])[None]  2.15 us
  transfers between devices with their start and end apart: 8, of which 4 were waited for; matrix products, arithmetic and copies ran while one was open for 0% of the time, Pallas kernels for 48%

profile of v2, /device:TPU:1, one launch (start us, length us, event | category | flops | bytes accessed | tf_op | source)
XLA Modules:
  0.0 50.6 jit_solution(3020357071278415105)
XLA Ops:
  0.7 2.5 %shard_map.140 = (bf16[512,512]{1,0:T(8,128)(2,1)S(1)}, bf16[1024,512]{1,0:T(8,128)(2,1)S(1)}, bf16[512,512]{1,0:T(8,128)(2,1)S(1)}, bf16[1024,512]{1,0:T(8,128)...) custom-call(bf16[1024,512]{1,0:T(8,128)(2,1)} %bitcast.22, ...), custom_call_target="tpu_custom_call" | custom-call | flops 536870912 | bytes 1048576 | tf_op jit(solution)/shard_map/pallas_call | solution.py:418
  3.2 4.5 %collective-permute-start.2 = (bf16[512,512]{1,0:T(8,128)(2,1)S(1)}, bf16[512,512]{1,0:T(8,128)(2,1)S(1)}, u32[]{:S(2)}, u32[]{:S(2)}) collective-permute-start(bf16[512,512]{1,0:T(8,128)(2,1)S(1)} %get-tuple-element.55), channel_id=1, source_target_pairs={{2,4},{4,2},{6,8},{8,6},{10,12},{12,10},{14,16},{16,14},{18,20},{2... | collective-permute-start | bytes 1572872 | tf_op jit(solution)/shard_map/ppermute | solution.py:430
  7.8 1.2 %shard_map.142 = (bf16[1024,512]{1,0:T(8,128)(2,1)S(1)}, bf16[256,512]{1,0:T(8,128)(2,1)S(1)}, bf16[256,512]{1,0:T(8,128)(2,1)S(1)}) custom-call(bf16[1024,512]{1,0:T(8,128)(2,1)S(1)} %get-tuple-element.49.mesh_ref, bf16[512,512]{1,0:T(8,128)(2,1)S(1)} %get-tuple-element.45.w_src_ref, s32[2,512]{1,0:T(2,128)S(1)} %copy-done.2), custom_call_target="tpu_custom_call" | custom-call | flops 1 | bytes 1 | tf_op jit(solution)/shard_map/pallas_call | solution.py:432
  9.0 0.1 collective-permute-start
  9.1 0.5 collective-permute-start.1
  9.6 1.7 %shard_map.141 = (f32[1024,512]{1,0:T(8,128)S(1)}, bf16[4,1024,512]{2,1,0:T(8,128)(2,1)S(1)}, bf16[2,512,2048]{2,1,0:T(8,128)(2,1)S(1)}, bf16[512,512]{1,0:T(8,1...) custom-call(s32[4,1024]{1,0:T(4,128)S(1)} %bitcast.10, ...), custom_call_target="tpu_custom_call" | custom-call | flops 1 | bytes 1 | tf_op jit(solution)/shard_map/pallas_call | solution.py:443
  11.3 7.8 %shard_map.143.pre_ref = bf16[4,1024,512]{2,1,0:T(8,128)(2,1)S(1)} custom-call(s32[4,1024]{1,0:T(4,128)S(1)} %bitcast.11, bf16[1024,512]{1,0:T(8,128)(2,1)S(1)} %get-tuple-element.50.src_ref, f32[1024,512]{1,0:T(8,128)S(1)} %get-tuple-element.51.dst_ref, bf16[4,4,1024]{2,1,0:T(4,128)(2,1)S(1)} %copy-done.3, bf16[4,512]{1,0:T(4,128)(2,1)S(1)} %copy-done.5, ...), custom_call_target="tpu_custom_call" | custom-call | flops 1 | bytes 1 | tf_op jit(solution)/shard_map/pallas_call | solution.py:460
  19.2 0.3 collective-permute-done.2.far_ref
  19.5 2.3 %shard_map.144 = (f32[128,512]{1,0:T(8,128)S(1)}, bf16[112,512]{1,0:T(8,128)(2,1)S(1)}, bf16[4,512,512]{2,1,0:T(8,128)(2,1)S(1)}, bf16[512,512]{1,0:T(8,128)(2,1)S(1)}, f32[512,128]{1,0:T(8,128)S(1)}) custom-call(bf16[4,1024,512]{2,1,0:T(8,128)(2,1)S(1)} %get-tuple-element.48.columns_ref, bf16[4,1024,512]{2,1,0:T(8,128)(2,1)S(1)} %shard_map.143.pre_ref, ...), custom_call_target="tpu_custom_call" | custom-call | flops 1342177280 | bytes 4194304 | tf_op jit(solution)/shard_map/pallas_call | solution.py:475
  21.7 1.3 %collective-permute-start.3 = (bf16[112,512]{1,0:T(8,128)(2,1)S(1)}, bf16[112,512]{1,0:T(8,128)(2,1)S(1)}, u32[]{:S(2)}, u32[]{:S(2)}) collective-permute-start(bf16[112,512]{1,0:T(8,128)(2,1)S(1)} %get-tuple-element.57), channel_id=1, source_target_pairs={{0,1},{1,0},{2,3},{3,2},{4,5},{5,4},{6,7},{7,6},{8,9},{9,8},{10,11... | collective-permute-start | bytes 344072 | tf_op jit(solution)/shard_map/ppermute | solution.py:490
  23.0 2.3 %shard_map.146 = (f32[128,512]{1,0:T(8,128)S(1)}, bf16[112,512]{1,0:T(8,128)(2,1)S(1)}, bf16[4,512,512]{2,1,0:T(8,128)(2,1)S(1)}, bf16[512,512]{1,0:T(8,128)(2,1)S(1)}, f32[512,128]{1,0:T(8,128)S(1)}) custom-call(bf16[4,1024,512]{2,1,0:T(8,128)(2,1)S(1)} %get-tuple-element.48.columns_ref, bf16[4,1024,512]{2,1,0:T(8,128)(2,1)S(1)} %shard_map.143.pre_ref, ...), custom_call_target="tpu_custom_call" | custom-call | flops 1342177280 | bytes 4194304 | tf_op jit(solution)/shard_map/pallas_call | solution.py:475
  25.3 0.3 collective-permute-start.4
  25.6 1.1 %collective-permute-done.3 = bf16[112,512]{1,0:T(8,128)(2,1)S(1)} collective-permute-done((bf16[112,512]{1,0:T(8,128)(2,1)S(1)}, bf16[112,512]{1,0:T(8,128)(2,1)S(1)}, u32[]{:S(2)}, u32[]{:S(2)}) %collective-permute-start.3) | collective-permute-done | bytes 114720 | tf_op jit(solution)/shard_map/ppermute | solution.py:490
  26.7 2.3 %shard_map.145 = (bf16[512,512]{1,0:T(8,128)(2,1)S(1)}, bf16[4,512,512]{2,1,0:T(8,128)(2,1)S(1)}, f32[512,512]{1,0:T(8,128)S(1)}) custom-call(bf16[2,512,2048]{2,1,0:T(8,128)(2,1)S(1)} %get-tuple-element.47.hot_ref, f32[128,512]{1,0:T(8,128)S(1)} %get-tuple-element.56.pred_ref, bf16[1,112,512]{2,1,0:T(8,128)(2,1)S(1)} %bitcast.15, ...), custom_call_target="tpu_custom_call" | custom-call | flops 1342177280 | bytes 4194304 | tf_op jit(solution)/shard_map/pallas_call | solution.py:500
  29.0 1.1 %collective-permute-done.4 = bf16[112,512]{1,0:T(8,128)(2,1)S(1)} collective-permute-done((bf16[112,512]{1,0:T(8,128)(2,1)S(1)}, bf16[112,512]{1,0:T(8,128)(2,1)S(1)}, u32[]{:S(2)}, u32[]{:S(2)}) %collective-permute-start.4) | collective-permute-done | bytes 114720 | tf_op jit(solution)/shard_map/ppermute | solution.py:490
  30.1 2.5 %shard_map.147 = (bf16[512,512]{1,0:T(8,128)(2,1)S(1)}, bf16[4,512,512]{2,1,0:T(8,128)(2,1)S(1)}, bf16[512,512]{1,0:T(8,128)(2,1)S(1)}) custom-call(bf16[2,512,2048]{2,1,0:T(8,128)(2,1)S(1)} %get-tuple-element.47.hot_ref, f32[128,512]{1,0:T(8,128)S(1)} %get-tuple-element.66.pred_ref, bf16[1,112,512]{2,1,0:T(8,128)(2,1)S(1)} %bitcast.14, ...), custom_call_target="tpu_custom_call" | custom-call | flops 1342177280 | bytes 4194304 | tf_op jit(solution)/shard_map/pallas_call | solution.py:500
  32.5 4.8 %collective-permute-start.7 = (bf16[512,512]{1,0:T(8,128)(2,1)S(1)}, bf16[512,512]{1,0:T(8,128)(2,1)S(1)}, u32[]{:S(2)}, u32[]{:S(2)}) collective-permute-start(bf16[512,512]{1,0:T(8,128)(2,1)S(1)} %get-tuple-element.81), channel_id=1, source_target_pairs={{2,4},{4,2},{6,8},{8,6},{10,12},{12,10},{14,16},{16,14},{18,20},{2... | collective-permute-start | bytes 1572872 | tf_op jit(solution)/shard_map/ppermute | solution.py:510
  37.3 2.3 %shard_map.149 = (bf16[256,512]{1,0:T(8,128)(2,1)S(1)}, bf16[256,512]{1,0:T(8,128)(2,1)S(1)}) custom-call(s32[4,1024]{1,0:T(4,128)S(1)} %bitcast.12, bf16[4,512,512]{2,1,0:T(8,128)(2,1)S(1)} %get-tuple-element.65.refs_1_.refs_0_, bf16[4,512,512]{2,1,0:T(8,128)(2,1)S(1)} %get-tuple-element.73.refs_3_.refs_1_), custom_call_target="tpu_custom_call" | custom-call | flops 1 | bytes 1 | tf_op jit(solution)/shard_map/pallas_call | solution.py:512
  39.6 0.1 collective-permute-start.5
  39.7 0.5 collective-permute-start.6
  40.2 5.1 %shard_map.148 = (bf16[1024,512]{1,0:T(8,128)(2,1)}, f32[1024,512]{1,0:T(8,128)S(1)}) custom-call(s32[4,1024]{1,0:T(4,128)S(1)} %bitcast.13, bf16[512,512]{1,0:T(8,128)(2,1)S(1)} %get-tuple-element.42.w_dst_ref, bf16[512,512]{1,0:T(8,128)(2,1)S(1)} %get-tuple-element.64.refs_0_, bf16[4,512,512]{2,1,0:T(8,128)(2,1)S(1)} %get-tuple-element.65.refs_1_.refs_0_, ...), custom_call_target="tpu_custom_call" | custom-call | flops 1 | bytes 1 | tf_op jit(solution)/shard_map/pallas_call | solution.py:522
  45.4 1.4 %shard_map.150 = (f32[1024,512]{1,0:T(8,128)S(1)}, bf16[1024,512]{1,0:T(8,128)(2,1)S(1)}) custom-call(s32[2,512]{1,0:T(2,128)S(1)} %copy-done.2, f32[1024,512]{1,0:T(8,128)S(1)} %get-tuple-element.75.own_ref, bf16[512,512]{1,0:T(8,128)(2,1)S(1)} %get-tuple-element.76.w_src_t_ref, bf16[256,512]{1,0:T(8,128)(2,1)S(1)} %collective-permute-done.5.refs_0_, ...), custom_call_target="tpu_custom_call" | custom-call | flops 1 | bytes 1 | tf_op jit(solution)/shard_map/pallas_call | solution.py:537
  46.7 1.8 %collective-permute-done.7.refs_0_ = bf16[512,512]{1,0:T(8,128)(2,1)S(1)} collective-permute-done((bf16[512,512]{1,0:T(8,128)(2,1)S(1)}, bf16[512,512]{1,0:T(8,128)(2,1)S(1)}, u32[]{:S(2)}, u32[]{:S(2)}) %collective-permute-start.7) | collective-permute-done | bytes 524320 | tf_op jit(solution)/shard_map/ppermute | solution.py:510
  48.6 1.8 %shard_map.151 = bf16[1024,512]{1,0:T(8,128)(2,1)} custom-call(bf16[1024,512]{1,0:T(8,128)(2,1)S(1)} %get-tuple-element.79.hot_ref, f32[1024,512]{1,0:T(8,128)S(1)} %get-tuple-element.80.base_ref, bf16[512,512]{1,0:T(8,128)(2,1)S(1)} %get-tuple-element.76.w_src_t_ref, bf16[512,512]{1,0:T(8,128)(2,1)S(1)} %collective-permute-done.7.refs_0_), custom_call_target="tpu_custom_call" | custom-call | flops 1073741824 | bytes 4194304 | tf_op jit(solution)/shard_map/pallas_call | solution.py:546
  (18 shorter events, 0.0 us)
Async XLA Ops:
  0.6 7.1 %copy-start.2 = (s32[2,512]{1,0:T(2,128)S(1)}, s32[2,512]{1,0:T(2,128)}, u32[]{:S(2)}) copy-start(s32[2,512]{1,0:T(2,128)} %send_ref.3) | copy-start | bytes 12292
  0.6 9.0 %copy-start = (s32[1024,4]{0,1:T(4,128)S(1)}, s32[1024,4]{0,1:T(4,128)}, u32[]{:S(2)}) copy-start(s32[1024,4]{0,1:T(4,128)} %param.16) | copy-start | bytes 49156
  0.7 8.9 %copy-start.1 = (bf16[512,100]{0,1:T(8,128)(2,1)S(1)}, bf16[512,100]{0,1:T(8,128)(2,1)}, u32[]{:S(2)}) copy-start(bf16[512,100]{0,1:T(8,128)(2,1)} %param.25) | copy-start | bytes 307204
  0.7 8.9 %copy-start.6 = (f32[100]{0:T(128)S(1)}, f32[100]{0:T(128)}, u32[]{:S(2)}) copy-start(f32[100]{0:T(128)} %param.19) | copy-start | bytes 1204
  3.2 16.3 %collective-permute-start.2 = (bf16[512,512]{1,0:T(8,128)(2,1)S(1)}, bf16[512,512]{1,0:T(8,128)(2,1)S(1)}, u32[]{:S(2)}, u32[]{:S(2)}) collective-permute-start(bf16[512,512]{1,0:T(8,128)(2,1)S(1)} %get-tuple-element.55), channel_id=1, source_target_pairs={{2,4},{4,2},{6,8},{8,6},{10,12},{12,10},{14,16},{16,14},{18,20},{2... | collective-permute-start | bytes 1572872 | tf_op jit(solution)/shard_map/ppermute | solution.py:430
  7.7 3.6 %copy-start.3 = (bf16[4,4,1024]{2,1,0:T(4,128)(2,1)S(1)}, bf16[4,4,1024]{2,1,0:T(4,128)(2,1)}, u32[]{:S(2)}) copy-start(bf16[4,4,1024]{2,1,0:T(4,128)(2,1)} %attr_ref.1) | copy-start | bytes 98308
  7.7 3.6 %copy-start.5 = (bf16[4,512]{1,0:T(4,128)(2,1)S(1)}, bf16[4,512]{1,0:T(4,128)(2,1)}, u32[]{:S(2)}) copy-start(bf16[4,512]{1,0:T(4,128)(2,1)} %w_edge_ref.1) | copy-start | bytes 12292
  9.0 2.3 %collective-permute-start = (bf16[256,512]{1,0:T(8,128)(2,1)S(1)}, bf16[256,512]{1,0:T(8,128)(2,1)S(1)}, u32[]{:S(2)}, u32[]{:S(2)}) collective-permute-start(bf16[256,512]{1,0:T(8,128)(2,1)S(1)} %get-tuple-element.52), channel_id=1, source_target_pairs={{0,2},{2,0},{4,6},{6,4},{8,10},{10,8},{12,14},{14,12},{16,18},{18,... | collective-permute-start | bytes 786440 | tf_op jit(solution)/shard_map/ppermute | solution.py:439
  9.1 2.2 %collective-permute-start.1 = (bf16[256,512]{1,0:T(8,128)(2,1)S(1)}, bf16[256,512]{1,0:T(8,128)(2,1)S(1)}, u32[]{:S(2)}, u32[]{:S(2)}) collective-permute-start(bf16[256,512]{1,0:T(8,128)(2,1)S(1)} %get-tuple-element.53), channel_id=1, source_target_pairs={{0,2},{2,0},{4,6},{6,4},{8,10},{10,8},{12,14},{14,12},{16,18},{18,... | collective-permute-start | bytes 786440 | tf_op jit(solution)/shard_map/ppermute | solution.py:439
  11.3 8.1 %copy-start.4 = (f32[512]{0:T(512)S(1)}, f32[512]{0:T(512)}, u32[]{:S(2)}) copy-start(f32[512]{0:T(512)} %param.24) | copy-start | bytes 6148
  21.7 5.0 %collective-permute-start.3 = (bf16[112,512]{1,0:T(8,128)(2,1)S(1)}, bf16[112,512]{1,0:T(8,128)(2,1)S(1)}, u32[]{:S(2)}, u32[]{:S(2)}) collective-permute-start(bf16[112,512]{1,0:T(8,128)(2,1)S(1)} %get-tuple-element.57), channel_id=1, source_target_pairs={{0,1},{1,0},{2,3},{3,2},{4,5},{5,4},{6,7},{7,6},{8,9},{9,8},{10,11... | collective-permute-start | bytes 344072 | tf_op jit(solution)/shard_map/ppermute | solution.py:490
  25.3 4.8 %collective-permute-start.4 = (bf16[112,512]{1,0:T(8,128)(2,1)S(1)}, bf16[112,512]{1,0:T(8,128)(2,1)S(1)}, u32[]{:S(2)}, u32[]{:S(2)}) collective-permute-start(bf16[112,512]{1,0:T(8,128)(2,1)S(1)} %get-tuple-element.67), channel_id=1, source_target_pairs={{0,1},{1,0},{2,3},{3,2},{4,5},{5,4},{6,7},{7,6},{8,9},{9,8},{10,11... | collective-permute-start | bytes 344072 | tf_op jit(solution)/shard_map/ppermute | solution.py:490
  32.5 16.1 %collective-permute-start.7 = (bf16[512,512]{1,0:T(8,128)(2,1)S(1)}, bf16[512,512]{1,0:T(8,128)(2,1)S(1)}, u32[]{:S(2)}, u32[]{:S(2)}) collective-permute-start(bf16[512,512]{1,0:T(8,128)(2,1)S(1)} %get-tuple-element.81), channel_id=1, source_target_pairs={{2,4},{4,2},{6,8},{8,6},{10,12},{12,10},{14,16},{16,14},{18,20},{2... | collective-permute-start | bytes 1572872 | tf_op jit(solution)/shard_map/ppermute | solution.py:510
  39.6 5.7 %collective-permute-start.5 = (bf16[256,512]{1,0:T(8,128)(2,1)S(1)}, bf16[256,512]{1,0:T(8,128)(2,1)S(1)}, u32[]{:S(2)}, u32[]{:S(2)}) collective-permute-start(bf16[256,512]{1,0:T(8,128)(2,1)S(1)} %get-tuple-element.77), channel_id=1, source_target_pairs={{0,2},{2,0},{4,6},{6,4},{8,10},{10,8},{12,14},{14,12},{16,18},{18,... | collective-permute-start | bytes 786440 | tf_op jit(solution)/shard_map/ppermute | solution.py:520
  39.7 5.7 %collective-permute-start.6 = (bf16[256,512]{1,0:T(8,128)(2,1)S(1)}, bf16[256,512]{1,0:T(8,128)(2,1)S(1)}, u32[]{:S(2)}, u32[]{:S(2)}) collective-permute-start(bf16[256,512]{1,0:T(8,128)(2,1)S(1)} %get-tuple-element.78), channel_id=1, source_target_pairs={{0,2},{2,0},{4,6},{6,4},{8,10},{10,8},{12,14},{14,12},{16,18},{18,... | collective-permute-start | bytes 786440 | tf_op jit(solution)/shard_map/ppermute | solution.py:520

commit v3 on v2

--- a/solution.py
+++ b/solution.py
@@ -117,39 +117,43 @@
         whole_ref[rows, :] = ref[...]
 
 
-def far_kernel(held, mesh_hbm, w_src_hbm, send_hbm, *refs):
-    held_hbm, (far_ref, mesh_ref, w_src_ref, *held_refs) = refs[:held], refs[held:-2]
-    send_ref, sems = refs[-2:]
+def far_kernel(mesh_hbm, w_src_hbm, send_hbm, far_ref, mesh_ref, w_src_ref, send_ref, sems):
     owned = mesh_ref.shape[0]
     parts = pieces(owned, owned // 2)
     moves = [(send_hbm, send_ref)]
     moves += [(mesh_hbm.at[part], mesh_ref.at[part]) for part in parts]
-    moves += [(w_src_hbm, w_src_ref), *zip(held_hbm, held_refs)]
+    moves += [(w_src_hbm, w_src_ref)]
     loads = [pltpu.make_async_copy(*move, sems.at[i]) for i, move in enumerate(moves)]
     for load in loads:
         load.start()
     loads[0].wait()
-    far = near_far(send_ref[0:1, :], send_ref[1:2, :])[1]
-    column = column_of(far)
+    column = column_of(near_far(send_ref[0:1, :], send_ref[1:2, :])[1])
     hots = [column_hot(column, part.start, part.stop - part.start) for part in parts]
     rows = None
     for load, part, hot in zip(loads[1:], parts, hots):
         load.wait()
         picked = mm(hot, mesh_ref[part])
         rows = picked if rows is None else rows + picked
-    loads[1 + len(parts)].wait()
+    loads[-1].wait()
     far_ref[...] = mm(rows.astype(BF16), w_src_ref[...]).astype(BF16)
-    for load in loads[2 + len(parts) :]:
-        load.wait()
-
-
-def near_kernel(mesh_ref, w_src_ref, send_ref, src_ref, *near_refs):
+
+
+def near_kernel(held, mesh_ref, w_src_ref, send_ref, *refs):
+    held_hbm, (src_ref, *near_refs), sems = refs[:held], refs[held : -held - 1], refs[-1]
+    loads = [
+        pltpu.make_async_copy(*move, sems.at[i])
+        for i, move in enumerate(zip(held_hbm, refs[-held - 1 : -1]))
+    ]
+    for load in loads:
+        load.start()
     src = mm(mesh_ref[...], w_src_ref[...]).astype(BF16)
     src_ref[...] = src
     near = near_far(send_ref[0:1, :], send_ref[1:2, :])[0]
     rows = mm(column_hot(column_of(near), 0, src.shape[0]), src_ref[...]).astype(BF16)
     for part, near_ref in placed_rows(near_refs):
         near_ref[...] = rows[part, :]
+    for load in loads:
+        load.wait()
 
 
 def ready_kernel(
@@ -414,28 +418,29 @@
 
     far_shapes = [sds((halo, channels), BF16)]
     near_shapes = [sds((halo // 2, channels), BF16)] * 2
-    held = [grid_rows, w_dst, w_msg, target]
-    *far, mesh_rows, w_src, grid_rows, w_dst, w_msg, target = call(
-        functools.partial(far_kernel, len(held)),
-        [far_memory] * (3 + len(held)),
-        [vmem] * (3 + len(held)),
-        far_shapes + [sds(array.shape, array.dtype) for array in (mesh_rows, w_src, *held)],
+    needed = [mesh_rows, w_src, send_rows]
+    *far, mesh_rows, w_src, send_rows = call(
+        far_kernel,
+        [far_memory] * 3,
+        [vmem] * 4,
+        far_shapes + [sds(array.shape, array.dtype) for array in needed],
         2 * owned * channels * halo,
         2 * owned * channels,
-        [
-            vmem((2, halo), jnp.int32),
-            pltpu.SemaphoreType.DMA((4 + len(held),)),
-        ],
-    )(*map(hbm, (mesh_rows, w_src, send_rows, *held)))
+        [pltpu.SemaphoreType.DMA((4,))],
+    )(*map(hbm, needed))
     far = [lax.ppermute(piece, "band", far_swap) for piece in far]
 
+    held = [grid_rows, w_dst, w_msg, target]
     src, *near = call(
-        near_kernel,
-        [vmem] * 3,
-        [vmem] * (1 + len(near_shapes)),
-        [sds((owned, channels), BF16), *near_shapes],
+        functools.partial(near_kernel, len(held)),
+        [vmem] * 3 + [far_memory] * len(held),
+        [vmem] * (1 + len(near_shapes) + len(held)),
+        [sds((owned, channels), BF16), *near_shapes]
+        + [sds(array.shape, array.dtype) for array in held],
         *IN_SHADOW,
-    )(mesh_rows, w_src, send_rows)
+        [pltpu.SemaphoreType.DMA((len(held),))],
+    )(mesh_rows, w_src, send_rows, *map(hbm, held))
+    *near, grid_rows, w_dst, w_msg, target = near
     near = [lax.ppermute(piece, "band", near_swap) for piece in near]
 
     chunks = 2

time: 51.1 us -> 51.2 us (level)
    pallas_call x2, Pallas kernels: 3.75 us -> 4.28 us  [the longest x1 2.4 us: per_device(): call(far_kernel, [far_memory] * 3, [vmem] * 4, far_shapes + [sds(array.sh...]
  transfers between devices with their start and end apart: 8 -> 8, of which waited for: 4 -> 3; matrix products, arithmetic and copies ran while one was open for 0% -> 0% of each run, Pallas kernels for 48% -> 49%
where the time goes in v3:
time: 51.2 us; the launch traced here: 51 us
  Pallas kernels  33.7 us (66%)
  starting transfers between devices  12.1 us (24%)
  waiting for transfers between devices  4.08 us (8%)
  between operations  1.01 us (2%)
    ppermute x2, starting transfers between devices, per_device(): far = [lax.ppermute(piece, 'band', far_swap) for piece in far]  9.39 us
    pallas_call x1, Pallas kernels, per_device(): call(functools.partial(own_kernel, block), [vmem] * (5 + len(near)), [vme...  7.81 us
    pallas_call x1, Pallas kernels, per_device(): call(functools.partial(own_grad_kernel, chunks), [vmem] * (2 + 2 * chunks...  5.14 us
    pallas_call x2, Pallas kernels, per_device(): call(functools.partial(backward_kernel, c, block, coeff, len(far)), [vmem...  4.73 us
    pallas_call x2, Pallas kernels, per_device(): call(functools.partial(forward_kernel, c * part, block), [vmem] * (6 + le...  4.55 us
    pallas_call x1, Pallas kernels, per_device(): call(far_kernel, [far_memory] * 3, [vmem] * 4, far_shapes + [sds(array.sh...  2.4 us
    pallas_call x1, Pallas kernels, per_device(): call(functools.partial(rim_kernel, owned, chunks), [vmem] * (1 + chunks),...  2.32 us
    ppermute x2, waiting for transfers between devices, per_device(): far = [lax.ppermute(piece, 'band', far_swap) for piece in far]  2.24 us
  transfers between devices with their start and end apart: 8, of which 3 were waited for; matrix products, arithmetic and copies ran while one was open for 0% of the time, Pallas kernels for 49%

profile of v3, /device:TPU:1, one launch (start us, length us, event | category | flops | bytes accessed | tf_op | source)
XLA Modules:
  0.0 51.0 jit_solution(15766840726972449203)
XLA Ops:
  0.6 2.4 %shard_map.140 = (bf16[512,512]{1,0:T(8,128)(2,1)S(1)}, bf16[1024,512]{1,0:T(8,128)(2,1)S(1)}, bf16[512,512]{1,0:T(8,128)(2,1)S(1)}, s32[2,512]{1,0:T(2,128)S(1)}) custom-call(bf16[1024,512]{1,0:T(8,128)(2,1)} %bitcast.24, bf16[512,512]{1,0:T(8,128)(2,1)} %w_src_hbm.1, s32[2,512]{1,0:T(2,128)} %send_hbm.1), custom_call_target="tpu_custom_call" | custom-call | flops 536870912 | bytes 1048576 | tf_op jit(solution)/shard_map/pallas_call | solution.py:422
  3.0 0.0 copy-start
  3.1 4.7 %collective-permute-start.2 = (bf16[512,512]{1,0:T(8,128)(2,1)S(1)}, bf16[512,512]{1,0:T(8,128)(2,1)S(1)}, u32[]{:S(2)}, u32[]{:S(2)}) collective-permute-start(bf16[512,512]{1,0:T(8,128)(2,1)S(1)} %get-tuple-element.57), channel_id=1, source_target_pairs={{2,4},{4,2},{6,8},{8,6},{10,12},{12,10},{14,16},{16,14},{18,20},{2... | collective-permute-start | bytes 1572872 | tf_op jit(solution)/shard_map/ppermute | solution.py:431
  7.7 1.9 %shard_map.141 = (bf16[1024,512]{1,0:T(8,128)(2,1)S(1)}, bf16[256,512]{1,0:T(8,128)(2,1)S(1)}, bf16[256,512]{1,0:T(8,128)(2,1)S(1)}, bf16[1024,512]{1,0:T(8,128)...) custom-call(bf16[1024,512]{1,0:T(8,128)(2,1)S(1)} %get-tuple-element.43.mesh_ref, ...), custom_call_target="tpu_custom_call" | custom-call | flops 1 | bytes 1 | tf_op jit(solution)/shard_map/pallas_call | solution.py:434
  9.7 0.1 collective-permute-start
  9.7 0.5 collective-permute-start.1
  10.2 1.7 %shard_map.142 = (f32[1024,512]{1,0:T(8,128)S(1)}, bf16[4,1024,512]{2,1,0:T(8,128)(2,1)S(1)}, bf16[2,512,2048]{2,1,0:T(8,128)(2,1)S(1)}, bf16[512,512]{1,0:T(8,1...) custom-call(s32[4,1024]{1,0:T(4,128)S(1)} %bitcast.10, ...), custom_call_target="tpu_custom_call" | custom-call | flops 1 | bytes 1 | tf_op jit(solution)/shard_map/pallas_call | solution.py:448
  12.0 7.8 %shard_map.143.pre_ref = bf16[4,1024,512]{2,1,0:T(8,128)(2,1)S(1)} custom-call(s32[4,1024]{1,0:T(4,128)S(1)} %bitcast.11, bf16[1024,512]{1,0:T(8,128)(2,1)S(1)} %get-tuple-element.52.src_ref, f32[1024,512]{1,0:T(8,128)S(1)} %get-tuple-element.53.dst_ref, bf16[4,4,1024]{2,1,0:T(4,128)(2,1)S(1)} %copy-done.2, bf16[4,512]{1,0:T(4,128)(2,1)S(1)} %copy-done.4, ...), custom_call_target="tpu_custom_call" | custom-call | flops 1 | bytes 1 | tf_op jit(solution)/shard_map/pallas_call | solution.py:465
  19.8 2.3 %shard_map.144 = (f32[128,512]{1,0:T(8,128)S(1)}, bf16[112,512]{1,0:T(8,128)(2,1)S(1)}, bf16[4,512,512]{2,1,0:T(8,128)(2,1)S(1)}, bf16[512,512]{1,0:T(8,128)(2,1)S(1)}, f32[512,128]{1,0:T(8,128)S(1)}) custom-call(bf16[4,1024,512]{2,1,0:T(8,128)(2,1)S(1)} %get-tuple-element.51.columns_ref, bf16[4,1024,512]{2,1,0:T(8,128)(2,1)S(1)} %shard_map.143.pre_ref, ...), custom_call_target="tpu_custom_call" | custom-call | flops 1342177280 | bytes 4194304 | tf_op jit(solution)/shard_map/pallas_call | solution.py:480
  22.1 1.3 %collective-permute-start.3 = (bf16[112,512]{1,0:T(8,128)(2,1)S(1)}, bf16[112,512]{1,0:T(8,128)(2,1)S(1)}, u32[]{:S(2)}, u32[]{:S(2)}) collective-permute-start(bf16[112,512]{1,0:T(8,128)(2,1)S(1)} %get-tuple-element.59), channel_id=1, source_target_pairs={{0,1},{1,0},{2,3},{3,2},{4,5},{5,4},{6,7},{7,6},{8,9},{9,8},{10,11... | collective-permute-start | bytes 344072 | tf_op jit(solution)/shard_map/ppermute | solution.py:495
  23.4 2.3 %shard_map.146 = (f32[128,512]{1,0:T(8,128)S(1)}, bf16[112,512]{1,0:T(8,128)(2,1)S(1)}, bf16[4,512,512]{2,1,0:T(8,128)(2,1)S(1)}, bf16[512,512]{1,0:T(8,128)(2,1)S(1)}, f32[512,128]{1,0:T(8,128)S(1)}) custom-call(bf16[4,1024,512]{2,1,0:T(8,128)(2,1)S(1)} %get-tuple-element.51.columns_ref, bf16[4,1024,512]{2,1,0:T(8,128)(2,1)S(1)} %shard_map.143.pre_ref, ...), custom_call_target="tpu_custom_call" | custom-call | flops 1342177280 | bytes 4194304 | tf_op jit(solution)/shard_map/pallas_call | solution.py:480
  25.7 0.3 collective-permute-start.4
  26.0 0.9 %collective-permute-done.3 = bf16[112,512]{1,0:T(8,128)(2,1)S(1)} collective-permute-done((bf16[112,512]{1,0:T(8,128)(2,1)S(1)}, bf16[112,512]{1,0:T(8,128)(2,1)S(1)}, u32[]{:S(2)}, u32[]{:S(2)}) %collective-permute-start.3) | collective-permute-done | bytes 114720 | tf_op jit(solution)/shard_map/ppermute | solution.py:495
  26.9 2.3 %shard_map.145 = (bf16[512,512]{1,0:T(8,128)(2,1)S(1)}, bf16[4,512,512]{2,1,0:T(8,128)(2,1)S(1)}, f32[512,512]{1,0:T(8,128)S(1)}) custom-call(bf16[2,512,2048]{2,1,0:T(8,128)(2,1)S(1)} %get-tuple-element.50.hot_ref, f32[128,512]{1,0:T(8,128)S(1)} %get-tuple-element.58.pred_ref, bf16[1,112,512]{2,1,0:T(8,128)(2,1)S(1)} %bitcast.15, ...), custom_call_target="tpu_custom_call" | custom-call | flops 1342177280 | bytes 4194304 | tf_op jit(solution)/shard_map/pallas_call | solution.py:505
  29.2 0.9 %collective-permute-done.4 = bf16[112,512]{1,0:T(8,128)(2,1)S(1)} collective-permute-done((bf16[112,512]{1,0:T(8,128)(2,1)S(1)}, bf16[112,512]{1,0:T(8,128)(2,1)S(1)}, u32[]{:S(2)}, u32[]{:S(2)}) %collective-permute-start.4) | collective-permute-done | bytes 114720 | tf_op jit(solution)/shard_map/ppermute | solution.py:495
  30.1 2.5 %shard_map.147 = (bf16[512,512]{1,0:T(8,128)(2,1)S(1)}, bf16[4,512,512]{2,1,0:T(8,128)(2,1)S(1)}, bf16[512,512]{1,0:T(8,128)(2,1)S(1)}) custom-call(bf16[2,512,2048]{2,1,0:T(8,128)(2,1)S(1)} %get-tuple-element.50.hot_ref, f32[128,512]{1,0:T(8,128)S(1)} %get-tuple-element.68.pred_ref, bf16[1,112,512]{2,1,0:T(8,128)(2,1)S(1)} %bitcast.14, ...), custom_call_target="tpu_custom_call" | custom-call | flops 1342177280 | bytes 4194304 | tf_op jit(solution)/shard_map/pallas_call | solution.py:505
  32.6 4.7 %collective-permute-start.7 = (bf16[512,512]{1,0:T(8,128)(2,1)S(1)}, bf16[512,512]{1,0:T(8,128)(2,1)S(1)}, u32[]{:S(2)}, u32[]{:S(2)}) collective-permute-start(bf16[512,512]{1,0:T(8,128)(2,1)S(1)} %get-tuple-element.83), channel_id=1, source_target_pairs={{2,4},{4,2},{6,8},{8,6},{10,12},{12,10},{14,16},{16,14},{18,20},{2... | collective-permute-start | bytes 1572872 | tf_op jit(solution)/shard_map/ppermute | solution.py:515
  37.3 2.3 %shard_map.149 = (bf16[256,512]{1,0:T(8,128)(2,1)S(1)}, bf16[256,512]{1,0:T(8,128)(2,1)S(1)}) custom-call(s32[4,1024]{1,0:T(4,128)S(1)} %bitcast.12, bf16[4,512,512]{2,1,0:T(8,128)(2,1)S(1)} %get-tuple-element.67.refs_1_.refs_0_, bf16[4,512,512]{2,1,0:T(8,128)(2,1)S(1)} %get-tuple-element.75.refs_3_.refs_1_), custom_call_target="tpu_custom_call" | custom-call | flops 1 | bytes 1 | tf_op jit(solution)/shard_map/pallas_call | solution.py:517
  39.6 0.1 collective-permute-start.5
  39.7 0.5 collective-permute-start.6
  40.2 5.1 %shard_map.148 = (bf16[1024,512]{1,0:T(8,128)(2,1)}, f32[1024,512]{1,0:T(8,128)S(1)}) custom-call(s32[4,1024]{1,0:T(4,128)S(1)} %bitcast.13, bf16[512,512]{1,0:T(8,128)(2,1)S(1)} %get-tuple-element.46.w_dst_ref, bf16[512,512]{1,0:T(8,128)(2,1)S(1)} %get-tuple-element.66.refs_0_, bf16[4,512,512]{2,1,0:T(8,128)(2,1)S(1)} %get-tuple-element.67.refs_1_.refs_0_, ...), custom_call_target="tpu_custom_call" | custom-call | flops 1 | bytes 1 | tf_op jit(solution)/shard_map/pallas_call | solution.py:527
  45.4 1.4 %shard_map.150 = (f32[1024,512]{1,0:T(8,128)S(1)}, bf16[1024,512]{1,0:T(8,128)(2,1)S(1)}) custom-call(s32[2,512]{1,0:T(2,128)S(1)} %get-tuple-element.45.send_ref, f32[1024,512]{1,0:T(8,128)S(1)} %get-tuple-element.77.own_ref, bf16[512,512]{1,0:T(8,128)(2,1)S(1)} %get-tuple-element.78.w_src_t_ref, bf16[256,512]{1,0:T(8,128)(2,1)S(1)} %collective-permute-done.5.refs_0_, ...), custom_call_target="tpu_custom_call" | custom-call | flops 1 | bytes 1 | tf_op jit(solution)/shard_map/pallas_call | solution.py:542
  46.7 2.2 %collective-permute-done.7.refs_0_ = bf16[512,512]{1,0:T(8,128)(2,1)S(1)} collective-permute-done((bf16[512,512]{1,0:T(8,128)(2,1)S(1)}, bf16[512,512]{1,0:T(8,128)(2,1)S(1)}, u32[]{:S(2)}, u32[]{:S(2)}) %collective-permute-start.7) | collective-permute-done | bytes 524320 | tf_op jit(solution)/shard_map/ppermute | solution.py:515
  49.0 1.8 %shard_map.151 = bf16[1024,512]{1,0:T(8,128)(2,1)} custom-call(bf16[1024,512]{1,0:T(8,128)(2,1)S(1)} %get-tuple-element.81.hot_ref, f32[1024,512]{1,0:T(8,128)S(1)} %get-tuple-element.82.base_ref, bf16[512,512]{1,0:T(8,128)(2,1)S(1)} %get-tuple-element.78.w_src_t_ref, bf16[512,512]{1,0:T(8,128)(2,1)S(1)} %collective-permute-done.7.refs_0_), custom_call_target="tpu_custom_call" | custom-call | flops 1073741824 | bytes 4194304 | tf_op jit(solution)/shard_map/pallas_call | solution.py:551
  (16 shorter events, 0.0 us)
Async XLA Ops:
  3.0 7.2 %copy-start = (s32[1024,4]{0,1:T(4,128)S(1)}, s32[1024,4]{0,1:T(4,128)}, u32[]{:S(2)}) copy-start(s32[1024,4]{0,1:T(4,128)} %param.16) | copy-start | bytes 49156
  3.0 7.2 %copy-start.1 = (bf16[512,100]{0,1:T(8,128)(2,1)S(1)}, bf16[512,100]{0,1:T(8,128)(2,1)}, u32[]{:S(2)}) copy-start(bf16[512,100]{0,1:T(8,128)(2,1)} %param.25) | copy-start | bytes 307204
  3.1 7.2 %copy-start.5 = (f32[100]{0:T(128)S(1)}, f32[100]{0:T(128)}, u32[]{:S(2)}) copy-start(f32[100]{0:T(128)} %param.19) | copy-start | bytes 1204
  3.1 16.7 %collective-permute-start.2 = (bf16[512,512]{1,0:T(8,128)(2,1)S(1)}, bf16[512,512]{1,0:T(8,128)(2,1)S(1)}, u32[]{:S(2)}, u32[]{:S(2)}) collective-permute-start(bf16[512,512]{1,0:T(8,128)(2,1)S(1)} %get-tuple-element.57), channel_id=1, source_target_pairs={{2,4},{4,2},{6,8},{8,6},{10,12},{12,10},{14,16},{16,14},{18,20},{2... | collective-permute-start | bytes 1572872 | tf_op jit(solution)/shard_map/ppermute | solution.py:431
  9.6 2.3 %copy-start.2 = (bf16[4,4,1024]{2,1,0:T(4,128)(2,1)S(1)}, bf16[4,4,1024]{2,1,0:T(4,128)(2,1)}, u32[]{:S(2)}) copy-start(bf16[4,4,1024]{2,1,0:T(4,128)(2,1)} %attr_ref.1) | copy-start | bytes 98308
  9.7 2.3 %copy-start.4 = (bf16[4,512]{1,0:T(4,128)(2,1)S(1)}, bf16[4,512]{1,0:T(4,128)(2,1)}, u32[]{:S(2)}) copy-start(bf16[4,512]{1,0:T(4,128)(2,1)} %w_edge_ref.1) | copy-start | bytes 12292
  9.7 2.3 %collective-permute-start = (bf16[256,512]{1,0:T(8,128)(2,1)S(1)}, bf16[256,512]{1,0:T(8,128)(2,1)S(1)}, u32[]{:S(2)}, u32[]{:S(2)}) collective-permute-start(bf16[256,512]{1,0:T(8,128)(2,1)S(1)} %get-tuple-element.54), channel_id=1, source_target_pairs={{0,2},{2,0},{4,6},{6,4},{8,10},{10,8},{12,14},{14,12},{16,18},{18,... | collective-permute-start | bytes 786440 | tf_op jit(solution)/shard_map/ppermute | solution.py:444
  9.7 2.2 %collective-permute-start.1 = (bf16[256,512]{1,0:T(8,128)(2,1)S(1)}, bf16[256,512]{1,0:T(8,128)(2,1)S(1)}, u32[]{:S(2)}, u32[]{:S(2)}) collective-permute-start(bf16[256,512]{1,0:T(8,128)(2,1)S(1)} %get-tuple-element.55), channel_id=1, source_target_pairs={{0,2},{2,0},{4,6},{6,4},{8,10},{10,8},{12,14},{14,12},{16,18},{18,... | collective-permute-start | bytes 786440 | tf_op jit(solution)/shard_map/ppermute | solution.py:444
  12.0 7.8 %copy-start.3 = (f32[512]{0:T(512)S(1)}, f32[512]{0:T(512)}, u32[]{:S(2)}) copy-start(f32[512]{0:T(512)} %param.24) | copy-start | bytes 6148
  22.1 4.8 %collective-permute-start.3 = (bf16[112,512]{1,0:T(8,128)(2,1)S(1)}, bf16[112,512]{1,0:T(8,128)(2,1)S(1)}, u32[]{:S(2)}, u32[]{:S(2)}) collective-permute-start(bf16[112,512]{1,0:T(8,128)(2,1)S(1)} %get-tuple-element.59), channel_id=1, source_target_pairs={{0,1},{1,0},{2,3},{3,2},{4,5},{5,4},{6,7},{7,6},{8,9},{9,8},{10,11... | collective-permute-start | bytes 344072 | tf_op jit(solution)/shard_map/ppermute | solution.py:495
  25.7 4.4 %collective-permute-start.4 = (bf16[112,512]{1,0:T(8,128)(2,1)S(1)}, bf16[112,512]{1,0:T(8,128)(2,1)S(1)}, u32[]{:S(2)}, u32[]{:S(2)}) collective-permute-start(bf16[112,512]{1,0:T(8,128)(2,1)S(1)} %get-tuple-element.69), channel_id=1, source_target_pairs={{0,1},{1,0},{2,3},{3,2},{4,5},{5,4},{6,7},{7,6},{8,9},{9,8},{10,11... | collective-permute-start | bytes 344072 | tf_op jit(solution)/shard_map/ppermute | solution.py:495
  32.6 16.4 %collective-permute-start.7 = (bf16[512,512]{1,0:T(8,128)(2,1)S(1)}, bf16[512,512]{1,0:T(8,128)(2,1)S(1)}, u32[]{:S(2)}, u32[]{:S(2)}) collective-permute-start(bf16[512,512]{1,0:T(8,128)(2,1)S(1)} %get-tuple-element.83), channel_id=1, source_target_pairs={{2,4},{4,2},{6,8},{8,6},{10,12},{12,10},{14,16},{16,14},{18,20},{2... | collective-permute-start | bytes 1572872 | tf_op jit(solution)/shard_map/ppermute | solution.py:515
  39.6 5.7 %collective-permute-start.5 = (bf16[256,512]{1,0:T(8,128)(2,1)S(1)}, bf16[256,512]{1,0:T(8,128)(2,1)S(1)}, u32[]{:S(2)}, u32[]{:S(2)}) collective-permute-start(bf16[256,512]{1,0:T(8,128)(2,1)S(1)} %get-tuple-element.79), channel_id=1, source_target_pairs={{0,2},{2,0},{4,6},{6,4},{8,10},{10,8},{12,14},{14,12},{16,18},{18,... | collective-permute-start | bytes 786440 | tf_op jit(solution)/shard_map/ppermute | solution.py:525
  39.7 5.7 %collective-permute-start.6 = (bf16[256,512]{1,0:T(8,128)(2,1)S(1)}, bf16[256,512]{1,0:T(8,128)(2,1)S(1)}, u32[]{:S(2)}, u32[]{:S(2)}) collective-permute-start(bf16[256,512]{1,0:T(8,128)(2,1)S(1)} %get-tuple-element.80), channel_id=1, source_target_pairs={{0,2},{2,0},{4,6},{6,4},{8,10},{10,8},{12,14},{14,12},{16,18},{18,... | collective-permute-start | bytes 786440 | tf_op jit(solution)/shard_map/ppermute | solution.py:525

commit v4 on v0

--- a/solution.py
+++ b/solution.py
@@ -292,7 +292,7 @@
                 dpre_ref[k, part, :] = d_act * sg_ref[k, part, :]
     far = mm(hot_ref[chunk], dpre_ref[...].reshape(edges * points, channels))
     if prior:
-        far = far + prior[0][...]
+        far = far + prior[0][...].astype(F32)
     far_ref[...] = far.astype(far_ref.dtype)
 
 
@@ -340,7 +340,7 @@
     near, far = near_far(send_ref[0:1, :], send_ref[1:2, :])
     fill_rows(near_hot, near, 0)
     total = own_ref[...] + mm(near_hot[...], near_ref[...])
-    base_ref[...] = mm_t(total.astype(BF16), w_src_ref[...])
+    base_ref[...] = mm_t(total.astype(BF16), w_src_ref[...]).astype(BF16)
     fill_rows(hot_ref, far, 0)
 
 
@@ -352,7 +352,7 @@
         rows_ref[i * size : (i + 1) * size, :] = mm_t(far_ref[...], w_src_ref[...]).astype(BF16)
     stores = []
     for i, part in enumerate(pieces(owned, owned // 4)):
-        out = base_ref[part, :] + mm(hot_ref[part, :], rows_ref[...])
+        out = base_ref[part, :].astype(F32) + mm(hot_ref[part, :], rows_ref[...])
         out_ref[part, :] = out.astype(BF16)
         stores.append(pltpu.make_async_copy(out_ref.at[part], mesh_hbm.at[part], sems.at[i]))
         stores[-1].start()
@@ -469,7 +469,7 @@
     far = []
     d_zs, d_pres = [], []
     for c, (pred, others, sg, zhat, rstd) in enumerate(ahead):
-        rim_shapes = far_shapes if c == chunks - 1 else [sds((halo, channels), F32)]
+        rim_shapes = far_shapes if c == chunks - 1 else [sds((halo, channels), BF16)]
         d_z, d_pre, *far = call(
             functools.partial(backward_kernel, c, block, coeff, len(far)),
             [vmem] * (11 + len(far)),
@@ -515,7 +515,7 @@
         merge_kernel,
         [vmem] * (3 + len(near)),
         [vmem] * 2,
-        [sds((owned, channels), F32), sds((owned, halo), BF16)],
+        [sds((owned, channels), BF16), sds((owned, halo), BF16)],
         *IN_SHADOW,
         [vmem((halo, channels), BF16), vmem((owned, halo), BF16)],
     )(send_rows, own, w_src, *near)

time: 51 us -> 51 us (level)
  no operation moved by 1% of the time
where the time goes in v4:
time: 51 us; the launch traced here: 50.8 us
  Pallas kernels  32.6 us (64%)
  starting transfers between devices  11.9 us (23%)
  waiting for transfers between devices  5.24 us (10%)
  between operations  1.03 us (2%)
    ppermute x2, starting transfers between devices, per_device(): far = [lax.ppermute(piece, 'band', far_swap) for piece in far]  9.2 us
    pallas_call x1, Pallas kernels, per_device(): call(functools.partial(own_kernel, block), [vmem] * (6 + len(near)), [vme...  8.94 us
    pallas_call x1, Pallas kernels, per_device(): call(functools.partial(own_grad_kernel, chunks), [vmem] * (2 + 2 * chunks...  5.11 us
    pallas_call x2, Pallas kernels, per_device(): call(functools.partial(backward_kernel, c, block, coeff, len(far)), [vmem...  4.74 us
    pallas_call x2, Pallas kernels, per_device(): call(functools.partial(forward_kernel, c * part, block, fields), [vmem] *...  4.54 us
    pallas_call x1, Pallas kernels, per_device(): call(functools.partial(far_kernel, len(held)), [far_memory] * (3 + len(he...  2.44 us
    pallas_call x1, Pallas kernels, per_device(): call(functools.partial(rim_kernel, owned, chunks), [vmem] * (1 + chunks),...  2.32 us
    ppermute x2, waiting for transfers between devices, per_device(): far = [lax.ppermute(piece, 'band', far_swap) for piece in far]  2.27 us
  transfers between devices with their start and end apart: 8, of which 5 were waited for; matrix products, arithmetic and copies ran while one was open for 0% of the time, Pallas kernels for 47%

profile of v4, /device:TPU:1, one launch (start us, length us, event | category | flops | bytes accessed | tf_op | source)
XLA Modules:
  0.0 50.8 jit_solution(2367051282555351017)
XLA Ops:
  0.7 2.4 %shard_map.140 = (bf16[512,512]{1,0:T(8,128)(2,1)S(1)}, bf16[1024,512]{1,0:T(8,128)(2,1)S(1)}, bf16[512,512]{1,0:T(8,128)(2,1)S(1)}, bf16[1024,512]{1,0:T(8,128)(2,1)S(1)}, bf16[512,512]{1,0:T(8,128)(2,1)S(1)}) custom-call(bf16[1024,512]{1,0:T(8,128)(2,1)} %bitcast.25, bf16[512,512]{1,0:T(8,128)(2,1)} %w_src_hbm.1, s32[2,512]{1,0:T(2,128)} %send_ref.3, ...), custom_call_target="tpu_custom_call" | custom-call | flops 536870912 | bytes 1048576 | tf_op jit(solution)/shard_map/pallas_call | solution.py:403
  3.1 4.5 %collective-permute-start.2 = (bf16[512,512]{1,0:T(8,128)(2,1)S(1)}, bf16[512,512]{1,0:T(8,128)(2,1)S(1)}, u32[]{:S(2)}, u32[]{:S(2)}) collective-permute-start(bf16[512,512]{1,0:T(8,128)(2,1)S(1)} %get-tuple-element.45), channel_id=1, source_target_pairs={{2,4},{4,2},{6,8},{8,6},{10,12},{12,10},{14,16},{16,14},{18,20},{2... | collective-permute-start | bytes 1572872 | tf_op jit(solution)/shard_map/ppermute | solution.py:415
  7.7 1.2 %shard_map.141 = (bf16[1024,512]{1,0:T(8,128)(2,1)S(1)}, bf16[256,512]{1,0:T(8,128)(2,1)S(1)}, bf16[256,512]{1,0:T(8,128)(2,1)S(1)}) custom-call(bf16[1024,512]{1,0:T(8,128)(2,1)S(1)} %get-tuple-element.36.mesh_ref, bf16[512,512]{1,0:T(8,128)(2,1)S(1)} %get-tuple-element.37.w_src_ref, s32[2,512]{1,0:T(2,128)S(1)} %copy-done.4), custom_call_target="tpu_custom_call" | custom-call | flops 1 | bytes 1 | tf_op jit(solution)/shard_map/pallas_call | solution.py:417
  9.0 0.1 collective-permute-start
  9.0 0.5 collective-permute-start.1
  9.5 1.0 %collective-permute-done.refs_0_ = bf16[256,512]{1,0:T(8,128)(2,1)S(1)} collective-permute-done((bf16[256,512]{1,0:T(8,128)(2,1)S(1)}, bf16[256,512]{1,0:T(8,128)(2,1)S(1)}, u32[]{:S(2)}, u32[]{:S(2)}) %collective-permute-start) | collective-permute-done | bytes 262176 | tf_op jit(solution)/shard_map/ppermute | solution.py:424
  10.6 0.4 collective-permute-done.1.refs_1_
  11.0 8.9 %shard_map.142 = (bf16[4,1024,512]{2,1,0:T(8,128)(2,1)S(1)}, bf16[4,1024,512]{2,1,0:T(8,128)(2,1)S(1)}, bf16[2,512,2048]{2,1,0:T(8,128)(2,1)S(1)}) custom-call(s32[4,1024]{1,0:T(4,128)S(1)} %bitcast.14, bf16[1024,512]{1,0:T(8,128)(2,1)S(1)} %get-tuple-element.38.src_ref, bf16[1024,512]{1,0:T(8,128)(2,1)S(1)} %get-tuple-element.39.grid_ref, ...), custom_call_target="tpu_custom_call" | custom-call | flops 1 | bytes 1 | tf_op jit(solution)/shard_map/pallas_call | solution.py:428
  19.9 2.3 %shard_map.143 = (f32[128,512]{1,0:T(8,128)S(1)}, bf16[112,512]{1,0:T(8,128)(2,1)S(1)}, bf16[4,512,512]{2,1,0:T(8,128)(2,1)S(1)}, bf16[512,512]{1,0:T(8,128)(2,1)S(1)}, f32[512,128]{1,0:T(8,128)S(1)}) custom-call(bf16[4,1024,512]{2,1,0:T(8,128)(2,1)S(1)} %get-tuple-element.43.columns_ref, bf16[4,1024,512]{2,1,0:T(8,128)(2,1)S(1)} %get-tuple-element.44.pre_ref, ...), custom_call_target="tpu_custom_call" | custom-call | flops 1342177280 | bytes 4194304 | tf_op jit(solution)/shard_map/pallas_call | solution.py:448
  22.2 1.3 %collective-permute-start.3 = (bf16[112,512]{1,0:T(8,128)(2,1)S(1)}, bf16[112,512]{1,0:T(8,128)(2,1)S(1)}, u32[]{:S(2)}, u32[]{:S(2)}) collective-permute-start(bf16[112,512]{1,0:T(8,128)(2,1)S(1)} %get-tuple-element.47), channel_id=1, source_target_pairs={{0,1},{1,0},{2,3},{3,2},{4,5},{5,4},{6,7},{7,6},{8,9},{9,8},{10,11... | collective-permute-start | bytes 344072 | tf_op jit(solution)/shard_map/ppermute | solution.py:463
  23.5 2.3 %shard_map.145 = (f32[128,512]{1,0:T(8,128)S(1)}, bf16[112,512]{1,0:T(8,128)(2,1)S(1)}, bf16[4,512,512]{2,1,0:T(8,128)(2,1)S(1)}, bf16[512,512]{1,0:T(8,128)(2,1)S(1)}, f32[512,128]{1,0:T(8,128)S(1)}) custom-call(bf16[4,1024,512]{2,1,0:T(8,128)(2,1)S(1)} %get-tuple-element.43.columns_ref, bf16[4,1024,512]{2,1,0:T(8,128)(2,1)S(1)} %get-tuple-element.44.pre_ref, ...), custom_call_target="tpu_custom_call" | custom-call | flops 1342177280 | bytes 4194304 | tf_op jit(solution)/shard_map/pallas_call | solution.py:448
  25.8 0.3 collective-permute-start.4
  26.1 0.8 %collective-permute-done.3 = bf16[112,512]{1,0:T(8,128)(2,1)S(1)} collective-permute-done((bf16[112,512]{1,0:T(8,128)(2,1)S(1)}, bf16[112,512]{1,0:T(8,128)(2,1)S(1)}, u32[]{:S(2)}, u32[]{:S(2)}) %collective-permute-start.3) | collective-permute-done | bytes 114720 | tf_op jit(solution)/shard_map/ppermute | solution.py:463
  26.9 2.4 %shard_map.144 = (bf16[512,512]{1,0:T(8,128)(2,1)S(1)}, bf16[4,512,512]{2,1,0:T(8,128)(2,1)S(1)}, bf16[512,512]{1,0:T(8,128)(2,1)S(1)}) custom-call(bf16[2,512,2048]{2,1,0:T(8,128)(2,1)S(1)} %get-tuple-element.42.hot_ref, f32[128,512]{1,0:T(8,128)S(1)} %get-tuple-element.46.pred_ref, bf16[1,112,512]{2,1,0:T(8,128)(2,1)S(1)} %bitcast.18, ...), custom_call_target="tpu_custom_call" | custom-call | flops 1342177280 | bytes 4194304 | tf_op jit(solution)/shard_map/pallas_call | solution.py:473
  29.4 0.8 %collective-permute-done.4 = bf16[112,512]{1,0:T(8,128)(2,1)S(1)} collective-permute-done((bf16[112,512]{1,0:T(8,128)(2,1)S(1)}, bf16[112,512]{1,0:T(8,128)(2,1)S(1)}, u32[]{:S(2)}, u32[]{:S(2)}) %collective-permute-start.4) | collective-permute-done | bytes 114720 | tf_op jit(solution)/shard_map/ppermute | solution.py:463
  30.1 2.3 %shard_map.146 = (bf16[512,512]{1,0:T(8,128)(2,1)S(1)}, bf16[4,512,512]{2,1,0:T(8,128)(2,1)S(1)}, bf16[512,512]{1,0:T(8,128)(2,1)S(1)}) custom-call(bf16[2,512,2048]{2,1,0:T(8,128)(2,1)S(1)} %get-tuple-element.42.hot_ref, f32[128,512]{1,0:T(8,128)S(1)} %get-tuple-element.53.pred_ref, bf16[1,112,512]{2,1,0:T(8,128)(2,1)S(1)} %bitcast.17, ...), custom_call_target="tpu_custom_call" | custom-call | flops 1342177280 | bytes 4194304 | tf_op jit(solution)/shard_map/pallas_call | solution.py:473
  32.4 4.7 %collective-permute-start.7 = (bf16[512,512]{1,0:T(8,128)(2,1)S(1)}, bf16[512,512]{1,0:T(8,128)(2,1)S(1)}, u32[]{:S(2)}, u32[]{:S(2)}) collective-permute-start(bf16[512,512]{1,0:T(8,128)(2,1)S(1)} %get-tuple-element.67), channel_id=1, source_target_pairs={{2,4},{4,2},{6,8},{8,6},{10,12},{12,10},{14,16},{16,14},{18,20},{2... | collective-permute-start | bytes 1572872 | tf_op jit(solution)/shard_map/ppermute | solution.py:487
  37.1 2.3 %shard_map.148 = (bf16[256,512]{1,0:T(8,128)(2,1)S(1)}, bf16[256,512]{1,0:T(8,128)(2,1)S(1)}) custom-call(s32[4,1024]{1,0:T(4,128)S(1)} %bitcast.15, bf16[4,512,512]{2,1,0:T(8,128)(2,1)S(1)} %get-tuple-element.52.refs_1_.refs_0_, bf16[4,512,512]{2,1,0:T(8,128)(2,1)S(1)} %get-tuple-element.60.refs_3_.refs_1_), custom_call_target="tpu_custom_call" | custom-call | flops 1 | bytes 1 | tf_op jit(solution)/shard_map/pallas_call | solution.py:489
  39.4 0.1 collective-permute-start.5
  39.5 0.5 collective-permute-start.6
  40.0 5.1 %shard_map.147 = (bf16[1024,512]{1,0:T(8,128)(2,1)}, f32[1024,512]{1,0:T(8,128)S(1)}) custom-call(s32[4,1024]{1,0:T(4,128)S(1)} %bitcast.16, bf16[512,512]{1,0:T(8,128)(2,1)S(1)} %get-tuple-element.35.w_dst_ref, bf16[512,512]{1,0:T(8,128)(2,1)S(1)} %get-tuple-element.51.refs_0_, bf16[4,512,512]{2,1,0:T(8,128)(2,1)S(1)} %get-tuple-element.52.refs_1_.refs_0_, ...), custom_call_target="tpu_custom_call" | custom-call | flops 1 | bytes 1 | tf_op jit(solution)/shard_map/pallas_call | solution.py:499
  45.2 1.4 %shard_map.149 = (bf16[1024,512]{1,0:T(8,128)(2,1)S(1)}, bf16[1024,512]{1,0:T(8,128)(2,1)S(1)}) custom-call(s32[2,512]{1,0:T(2,128)S(1)} %copy-done.4, f32[1024,512]{1,0:T(8,128)S(1)} %get-tuple-element.62.own_ref, bf16[512,512]{1,0:T(8,128)(2,1)S(1)} %get-tuple-element.37.w_src_ref, bf16[256,512]{1,0:T(8,128)(2,1)S(1)} %collective-permute-done.5.refs_0_, ...), custom_call_target="tpu_custom_call" | custom-call | flops 1 | bytes 1 | tf_op jit(solution)/shard_map/pallas_call | solution.py:514
  46.5 2.3 %collective-permute-done.7.refs_0_ = bf16[512,512]{1,0:T(8,128)(2,1)S(1)} collective-permute-done((bf16[512,512]{1,0:T(8,128)(2,1)S(1)}, bf16[512,512]{1,0:T(8,128)(2,1)S(1)}, u32[]{:S(2)}, u32[]{:S(2)}) %collective-permute-start.7) | collective-permute-done | bytes 524320 | tf_op jit(solution)/shard_map/ppermute | solution.py:487
  48.8 1.8 %shard_map.150 = bf16[1024,512]{1,0:T(8,128)(2,1)} custom-call(bf16[1024,512]{1,0:T(8,128)(2,1)S(1)} %get-tuple-element.65.hot_ref, bf16[1024,512]{1,0:T(8,128)(2,1)S(1)} %get-tuple-element.66.base_ref, bf16[512,512]{1,0:T(8,128)(2,1)S(1)} %get-tuple-element.37.w_src_ref, bf16[512,512]{1,0:T(8,128)(2,1)S(1)} %collective-permute-done.7.refs_0_), custom_call_target="tpu_custom_call" | custom-call | flops 1073741824 | bytes 4194304 | tf_op jit(solution)/shard_map/pallas_call | solution.py:523
  (21 shorter events, 0.1 us)
Async XLA Ops:
  0.6 7.0 %copy-start.4 = (s32[2,512]{1,0:T(2,128)S(1)}, s32[2,512]{1,0:T(2,128)}, u32[]{:S(2)}) copy-start(s32[2,512]{1,0:T(2,128)} %send_ref.3) | copy-start | bytes 12292
  0.6 10.3 %copy-start.3 = (s32[1024,4]{0,1:T(4,128)S(1)}, s32[1024,4]{0,1:T(4,128)}, u32[]{:S(2)}) copy-start(s32[1024,4]{0,1:T(4,128)} %param.16) | copy-start | bytes 49156
  0.7 10.3 %copy-start.5 = (bf16[4,4,1024]{2,1,0:T(4,128)(2,1)S(1)}, bf16[4,4,1024]{2,1,0:T(4,128)(2,1)}, u32[]{:S(2)}) copy-start(bf16[4,4,1024]{2,1,0:T(4,128)(2,1)} %attr_ref.1) | copy-start | bytes 98308
  0.7 10.3 %copy-start.7 = (bf16[4,512]{1,0:T(4,128)(2,1)S(1)}, bf16[4,512]{1,0:T(4,128)(2,1)}, u32[]{:S(2)}) copy-start(bf16[4,512]{1,0:T(4,128)(2,1)} %w_edge_ref.1) | copy-start | bytes 12292
  3.1 16.8 %collective-permute-start.2 = (bf16[512,512]{1,0:T(8,128)(2,1)S(1)}, bf16[512,512]{1,0:T(8,128)(2,1)S(1)}, u32[]{:S(2)}, u32[]{:S(2)}) collective-permute-start(bf16[512,512]{1,0:T(8,128)(2,1)S(1)} %get-tuple-element.45), channel_id=1, source_target_pairs={{2,4},{4,2},{6,8},{8,6},{10,12},{12,10},{14,16},{16,14},{18,20},{2... | collective-permute-start | bytes 1572872 | tf_op jit(solution)/shard_map/ppermute | solution.py:415
  7.7 12.2 %copy-start = (bf16[512,512]{1,0:T(8,128)(2,1)S(1)}, bf16[512,512]{1,0:T(8,128)(2,1)}, u32[]{:S(2)}) copy-start(bf16[512,512]{1,0:T(8,128)(2,1)} %w_msg_ref.7) | copy-start | bytes 1572868
  7.7 12.2 %copy-start.2 = (bf16[512,100]{0,1:T(8,128)(2,1)S(1)}, bf16[512,100]{0,1:T(8,128)(2,1)}, u32[]{:S(2)}) copy-start(bf16[512,100]{0,1:T(8,128)(2,1)} %param.25) | copy-start | bytes 307204
  7.7 12.2 %copy-start.6 = (f32[512]{0:T(512)S(1)}, f32[512]{0:T(512)}, u32[]{:S(2)}) copy-start(f32[512]{0:T(512)} %param.24) | copy-start | bytes 6148
  9.0 1.6 %collective-permute-start = (bf16[256,512]{1,0:T(8,128)(2,1)S(1)}, bf16[256,512]{1,0:T(8,128)(2,1)S(1)}, u32[]{:S(2)}, u32[]{:S(2)}) collective-permute-start(bf16[256,512]{1,0:T(8,128)(2,1)S(1)} %get-tuple-element.40), channel_id=1, source_target_pairs={{0,2},{2,0},{4,6},{6,4},{8,10},{10,8},{12,14},{14,12},{16,18},{18,... | collective-permute-start | bytes 786440 | tf_op jit(solution)/shard_map/ppermute | solution.py:424
  9.0 1.9 %collective-permute-start.1 = (bf16[256,512]{1,0:T(8,128)(2,1)S(1)}, bf16[256,512]{1,0:T(8,128)(2,1)S(1)}, u32[]{:S(2)}, u32[]{:S(2)}) collective-permute-start(bf16[256,512]{1,0:T(8,128)(2,1)S(1)} %get-tuple-element.41), channel_id=1, source_target_pairs={{0,2},{2,0},{4,6},{6,4},{8,10},{10,8},{12,14},{14,12},{16,18},{18,... | collective-permute-start | bytes 786440 | tf_op jit(solution)/shard_map/ppermute | solution.py:424
  22.2 4.7 %copy-start.1 = (f32[100,1024]{1,0:T(8,128)S(1)}, f32[100,1024]{1,0:T(8,128)}, u32[]{:S(2)}) copy-start(f32[100,1024]{1,0:T(8,128)} %target_ref.3) | copy-start | bytes 1228804
  22.2 4.7 %copy-start.8 = (f32[100]{0:T(128)S(1)}, f32[100]{0:T(128)}, u32[]{:S(2)}) copy-start(f32[100]{0:T(128)} %param.19) | copy-start | bytes 1204
  22.2 4.7 %collective-permute-start.3 = (bf16[112,512]{1,0:T(8,128)(2,1)S(1)}, bf16[112,512]{1,0:T(8,128)(2,1)S(1)}, u32[]{:S(2)}, u32[]{:S(2)}) collective-permute-start(bf16[112,512]{1,0:T(8,128)(2,1)S(1)} %get-tuple-element.47), channel_id=1, source_target_pairs={{0,1},{1,0},{2,3},{3,2},{4,5},{5,4},{6,7},{7,6},{8,9},{9,8},{10,11... | collective-permute-start | bytes 344072 | tf_op jit(solution)/shard_map/ppermute | solution.py:463
  25.8 4.3 %collective-permute-start.4 = (bf16[112,512]{1,0:T(8,128)(2,1)S(1)}, bf16[112,512]{1,0:T(8,128)(2,1)S(1)}, u32[]{:S(2)}, u32[]{:S(2)}) collective-permute-start(bf16[112,512]{1,0:T(8,128)(2,1)S(1)} %get-tuple-element.54), channel_id=1, source_target_pairs={{0,1},{1,0},{2,3},{3,2},{4,5},{5,4},{6,7},{7,6},{8,9},{9,8},{10,11... | collective-permute-start | bytes 344072 | tf_op jit(solution)/shard_map/ppermute | solution.py:463
  32.4 16.4 %collective-permute-start.7 = (bf16[512,512]{1,0:T(8,128)(2,1)S(1)}, bf16[512,512]{1,0:T(8,128)(2,1)S(1)}, u32[]{:S(2)}, u32[]{:S(2)}) collective-permute-start(bf16[512,512]{1,0:T(8,128)(2,1)S(1)} %get-tuple-element.67), channel_id=1, source_target_pairs={{2,4},{4,2},{6,8},{8,6},{10,12},{12,10},{14,16},{16,14},{18,20},{2... | collective-permute-start | bytes 1572872 | tf_op jit(solution)/shard_map/ppermute | solution.py:487
  39.4 5.7 %collective-permute-start.5 = (bf16[256,512]{1,0:T(8,128)(2,1)S(1)}, bf16[256,512]{1,0:T(8,128)(2,1)S(1)}, u32[]{:S(2)}, u32[]{:S(2)}) collective-permute-start(bf16[256,512]{1,0:T(8,128)(2,1)S(1)} %get-tuple-element.63), channel_id=1, source_target_pairs={{0,2},{2,0},{4,6},{6,4},{8,10},{10,8},{12,14},{14,12},{16,18},{18,... | collective-permute-start | bytes 786440 | tf_op jit(solution)/shard_map/ppermute | solution.py:497
  39.5 5.6 %collective-permute-start.6 = (bf16[256,512]{1,0:T(8,128)(2,1)S(1)}, bf16[256,512]{1,0:T(8,128)(2,1)S(1)}, u32[]{:S(2)}, u32[]{:S(2)}) collective-permute-start(bf16[256,512]{1,0:T(8,128)(2,1)S(1)} %get-tuple-element.64), channel_id=1, source_target_pairs={{0,2},{2,0},{4,6},{6,4},{8,10},{10,8},{12,14},{14,12},{16,18},{18,... | collective-permute-start | bytes 786440 | tf_op jit(solution)/shard_map/ppermute | solution.py:497
